TPU v7x, 32 devices: a whole 2x2x4 slice. The times are simulated.
32 devices in a mesh: row: 8 (over z, core), col: 4 (over y, x).
Axes of the slice: x: 2, y: 2, z: 4, core: 2. Of those that a mesh axis runs over, the one named last changes fastest.
Arguments:
- stiffness: bfloat16 [256, 16, 128, 128], P('row', 'col'), may hold values from -2.5 to 2.5
- stiff_columns: int32 [256, 16], P('row', 'col'), may hold values from 0 to 255, as said below
- stiff_stored: int32 [256, 16], P('row', 'col'), may hold values from 0 to 1, as said below
- prolongator: bfloat16 [256, 2, 128, 128], P(('row', 'col')), may hold values from -0.5 to 0.5
- prolong_columns: int32 [256, 2], replicated, may hold values from 0 to 31, as said below
Outputs:
- coarse_matrix: float32 [32, 32, 128, 128], P('row', 'col')
Inputs may be any that keep to these rules, and one draw needn't show every extreme that they name: `stiff_columns`: slots q * 4 to q * 4 + 3 of every row name fine block columns q * 64 to (q + 1) * 64 - 1. `stiff_stored`: each row range of 32 rows has its own share of stored slots, and in every draw one such range has all of its slots stored. `prolong_columns`: column 0 is the aggregate of fine block row i; each aggregate holds exactly 8 fine block rows, all in one row range of 32 rows, and the aggregates of range q are q * 4 to q * 4 + 3; column 1 is another aggregate of the same range.
All inputs are finite; a program needn't handle non-finite values.
Results may differ from a plain program's by a relative error of at most 0.0029.
Values may be sent and summed in bfloat16 or wider, within the bound.
No kernel may reach another device: no remote copies, remote signals or barrier semaphores. Data moves between devices by JAX's collectives and lax.ppermute only.
A program may use at most 256 MiB of HBM per device.

v0:
```python
import math

import jax
import jax.numpy as jnp
from jax import lax
from jax.sharding import PartitionSpec as P

G = 8


def broadcast(value, axis, source):
    kept = jnp.where(lax.axis_index(axis) == source, value, 0).astype(value.dtype)
    return lax.psum(kept, axis)


def shards(stiffness, stiff_columns, stiff_stored, prolongator, prolong_columns):
    rows_count = stiffness.shape[0]
    block_size = stiffness.shape[2]
    row_count = lax.axis_size("row")
    col_count = lax.axis_size("col")
    row_ratio = row_count // col_count
    row_pos = lax.axis_index("row")
    col_pos = lax.axis_index("col")
    agg_rows = rows_count // G
    agg_cols = row_ratio * agg_rows
    left_rows = lax.all_gather(prolongator, "col", axis=0, tiled=True)
    first_fine = col_pos * (row_ratio * rows_count)
    panels = [
        broadcast(left_rows, "row", col_pos * row_ratio + member) for member in range(row_ratio)
    ]
    right_rows = jnp.concatenate(panels, axis=0)
    right_index = stiff_columns - first_fine
    row_start = row_pos * rows_count
    left_ids = (
        lax.dynamic_slice_in_dim(prolong_columns, row_start, rows_count, 0) - row_pos * agg_rows
    )
    right_ids = prolong_columns[stiff_columns] - col_pos * agg_cols
    left_hot = (
        left_ids[:, :, None] == jnp.arange(agg_rows, dtype=jnp.int32)[None, None, :]
    ).astype(jnp.float32)
    right_hot = (
        right_ids[:, :, :, None] == jnp.arange(agg_cols, dtype=jnp.int32)[None, None, None, :]
    ).astype(jnp.bfloat16)
    row_step = math.gcd(rows_count, 16)

    def one_block(counter, coarse):
        first_row = counter * row_step
        stiff_rows = lax.dynamic_slice_in_dim(stiffness, first_row, row_step, 0)
        index_rows = lax.dynamic_slice_in_dim(right_index, first_row, row_step, 0)
        live_mask = lax.dynamic_slice_in_dim(stiff_stored, first_row, row_step, 0)
        left_block = lax.dynamic_slice_in_dim(left_rows, first_row, row_step, 0)
        left_onehot = lax.dynamic_slice_in_dim(left_hot, first_row, row_step, 0)
        right_onehot = lax.dynamic_slice_in_dim(right_hot, first_row, row_step, 0)
        right_block = right_rows[index_rows]
        product = jnp.einsum(
            "isxy,isbyz->isbxz", stiff_rows, right_block, preferred_element_type=jnp.float32
        )
        product = (product * live_mask[:, :, None, None, None].astype(jnp.float32)).astype(
            jnp.bfloat16
        )
        collected = jnp.einsum(
            "isbxz,isbj->ijxz", product, right_onehot, preferred_element_type=jnp.float32
        )
        projected = jnp.einsum(
            "iayx,ijyz->iajxz",
            left_block.astype(jnp.float32),
            collected,
            precision=lax.Precision.HIGHEST,
        )
        summed = jnp.einsum(
            "iajxz,iak->kjxz", projected, left_onehot, precision=lax.Precision.HIGHEST
        )
        return coarse + summed

    start_value = jnp.zeros((agg_rows, agg_cols, block_size, block_size), jnp.float32)
    return lax.fori_loop(0, rows_count // row_step, one_block, start_value)


def solution(mesh):
    return jax.shard_map(
        shards,
        mesh=mesh,
        in_specs=(
            P("row", "col", None, None),
            P("row", "col"),
            P("row", "col"),
            P(("row", "col"), None, None, None),
            P(),
        ),
        out_specs=P("row", "col", None, None),
        check_vma=False,
    )
```

profile of v0, /device:TPU:5, one launch (start us, length us, event | category | flops | bytes accessed | tf_op | source)
XLA Modules:
  0.0 291.5 jit_solution(18226481441169784379)
XLA Ops:
  6.5 0.7 all-gather.2.cloned.1.call-update
  7.3 38.4 %all-gather.2.cloned.1.call-done = bf16[32,2,128,128]{3,2,1,0:T(8,128)(2,1)} async-done(((bf16[8,2,128,128]{3,2,1,0:T(8,128)(2,1)}), bf16[32,2,128,128]{3,2,1,0:T(8,128)(2,1)}) %all-gather.2.cloned.1.call-update) | async-done | bytes 2097168 | tf_op jit(solution)/shard_map/all_gather | solution.py:26
  45.7 3.9 %broadcast_select_fusion.1 = (bf16[32,2,128,128]{3,2,1,0:T(8,128)(2,1)}, bf16[32,2,128,128]{3,2,1,0:T(8,128)(2,1)}) fusion(bf16[32,2,128,128]{3,2,1,0:T(8,128)(2,1)} %all-gather.2.cloned.1.call-done, pred[]{:T(512)S(6)} %eq.38, pred[]{:T(512)S(6)} %eq.39), kind=kLoop, calls=%fused_computation.25 | loop fusion | flops 2097152 | bytes 6291458 | tf_op jit(solution)/shard_map/jit(_where)/select_n | solution.py:12
  49.7 0.1 copy.23
  49.8 0.1 copy.25
  49.9 0.1 copy.22
  50.0 0.1 reshape.16
  50.1 0.6 gather_fusion.1
  50.8 0.3 copy.24
  51.2 0.1 fusion.14
  51.3 95.3 %all-reduce.3.cloned.1.call-done = (bf16[32,2,128,128]{3,2,1,0:T(8,128)(2,1)}, bf16[32,2,128,128]{3,2,1,0:T(8,128)(2,1)}) async-done(((bf16[32,2,128,128]{3,2,1,0:T(8,128)(2,1)}, bf16[32,2,128,128]{3,2,1,0:T(8,128)(2,1)}), (bf16[32,2,128,128]{3,2,1,0:T(8,128)(2,1)}, bf16[32,2,128,128]{3,2,1,0:T(8,128)(2,1)})) %all-reduce.3.cloned.1.call-update) | async-done | bytes 4194320 | tf_op jit(solution)/shard_map/psum | solution.py:13
  146.7 4.7 %pad_maximum_fusion = bf16[64,2,128,128]{3,2,1,0:T(8,128)(2,1)} fusion(bf16[32,2,128,128]{3,2,1,0:T(8,128)(2,1)} %get-tuple-element.217, bf16[32,2,128,128]{3,2,1,0:T(8,128)(2,1)} %get-tuple-element.218), kind=kLoop, calls=%fused_computation.23 | loop fusion | flops 2097152 | bytes 8388608 | tf_op jit(solution)/shard_map/concatenate | solution.py:31
  151.3 131.8 %while.14 = (s32[]{:T(128)}, f32[4,8,128,128]{3,0,2,1:T(4,128)S(1)}, f32[32,2,4]{0,2,1:T(4,128)S(1)}, bf16[32,4,2,8]{3,1,2,0:T(4,128)(2,1)S(1)}, s32[32,4]{1,0:T...) while((s32[]{:T(128)}, ...), condition=%wide.region_3.4_spmd.clone, body=%wide.region_2.3_spmd.clone.sunk | while | flops 7219446784 | bytes 120627664 | solution.py:76
  151.3 0.1 reshape.44
  151.4 5.2 %gather_fusion = bf16[64,2,128,128]{3,2,1,0:T(8,128)(2,1)} fusion(bf16[64,2,128,128]{3,2,1,0:T(8,128)(2,1)} %get-tuple-element.307, s32[1024]{0:T(1024)S(1)} %pad_clamp_fusion.3), kind=kCustom, calls=%fused_computation.clone.clone.1 | custom fusion | bytes 8388864 | tf_op jit(solution)/shard_map/while/body/eval_jaxpr/gather | solution.py:54
  156.7 0.1 copy.46
  156.8 6.7 %fusion.36 = bf16[16,4,2,128,128]{3,4,2,1,0:T(8,128)(2,1)} fusion(f32[16,4]{1,0:T(8,128)S(1)} %convert_element_type.43, bf16[16,4,2,128,128]{4,3,2,1,0:T(8,128)(2,1)} %bitcast.61, bf16[32,4,128,128]{3,2,1,0:T(8,128)(2,1)} %get-tuple-element.308, s32[]{:T(128)S(6)} %select_n.56), kind=kOutput, calls=%fused_computation.5.clone.1 | convolution fusion | flops 541065216 | bytes 10486020 | tf_op jit(solution)/shard_map/while/body/eval_jaxpr/isxy,isbyz->isbxz/dot_general | solution.py:55
  163.5 7.5 %copy.47 = bf16[16,4,2,128,128]{4,1,2,3,0:T(4,128)(2,1)} copy(bf16[16,4,2,128,128]{3,4,2,1,0:T(8,128)(2,1)} %fusion.36) | data formatting | bytes 8388608 | tf_op jit(solution)/shard_map/while/body/eval_jaxpr/convert_element_type | solution.py:58
  171.0 4.5 %convolution_bitcast_fusion.4 = f32[16,8,128,128,1]{3,1,2,0,4:T(8,128)S(1)} fusion(bf16[16,4,2,128,128]{4,1,2,3,0:T(4,128)(2,1)} %copy.47, bf16[32,4,2,8]{3,1,2,0:T(4,128)(2,1)S(1)} %get-tuple-element.305, s32[]{:T(128)S(6)} %select_n.56), kind=kOutput, calls=%fused_computation.6.clone.1 | convolution fusion | flops 33554432 | bytes 12615684 | tf_op jit(solution)/shard_map/while/body/eval_jaxpr/isbxz,isbj->ijxz/dot_general | solution.py:61
  175.5 11.6 %convolution_bitcast_fusion.5 = f32[16,2,8,128,128]{3,4,1,2,0:T(8,128)} fusion(f32[16,8,128,128,1]{3,1,2,0,4:T(8,128)S(1)} %convolution_bitcast_fusion.4, bf16[32,2,128,128]{3,2,1,0:T(8,128)(2,1)} %get-tuple-element.310, s32[]{:T(128)S(6)} %select_n.56), kind=kOutput, calls=%fused_computation.2.clone.1 | convolution fusion | flops 6442450944 | bytes 26214404 | tf_op jit(solution)/shard_map/while/body/eval_jaxpr/iayx,ijyz->iajxz/dot_general | solution.py:64
  187.1 17.5 %copy.48 = f32[16,2,8,128,128]{4,0,1,3,2:T(8,128)} copy(f32[16,2,8,128,128]{3,4,1,2,0:T(8,128)} %convolution_bitcast_fusion.5) | data formatting | bytes 33554432 | tf_op jit(solution)/shard_map/while/body/eval_jaxpr/iayx,ijyz->iajxz/transpose | solution.py:64
  204.6 12.6 %bitcast_add_fusion.2 = f32[4,8,128,128]{3,0,2,1:T(4,128)S(1)} fusion(f32[4,8,128,128]{3,0,2,1:T(4,128)S(1)} %get-tuple-element.290, f32[16,2,8,128,128]{4,0,1,3,2:T(8,128)} %copy.48, pred[]{:T(512)S(6)} %compare.3, f32[32,2,4]{0,2,1:T(4,128)S(1)} %get-tuple-element.304, s32[]{:T(128)S(6)} %select_n.56), kind=kOutput, calls=%fused_computation.8.clone.1 | convolution fusion | flops 202375168 | bytes 20972548 | tf_op jit(solution)/shard_map/while/body/eval_jaxpr/iajxz,iak->kjxz/dot_general | solution.py:70
  217.2 0.1 reshape.44
  217.3 5.2 %gather_fusion = bf16[64,2,128,128]{3,2,1,0:T(8,128)(2,1)} fusion(bf16[64,2,128,128]{3,2,1,0:T(8,128)(2,1)} %get-tuple-element.307, s32[1024]{0:T(1024)S(1)} %pad_clamp_fusion.3), kind=kCustom, calls=%fused_computation.clone.clone.1 | custom fusion | bytes 8388864 | tf_op jit(solution)/shard_map/while/body/eval_jaxpr/gather | solution.py:54
  222.6 0.1 copy.46
  222.7 6.7 %fusion.36 = bf16[16,4,2,128,128]{3,4,2,1,0:T(8,128)(2,1)} fusion(f32[16,4]{1,0:T(8,128)S(1)} %convert_element_type.43, bf16[16,4,2,128,128]{4,3,2,1,0:T(8,128)(2,1)} %bitcast.61, bf16[32,4,128,128]{3,2,1,0:T(8,128)(2,1)} %get-tuple-element.308, s32[]{:T(128)S(6)} %select_n.56), kind=kOutput, calls=%fused_computation.5.clone.1 | convolution fusion | flops 541065216 | bytes 10486020 | tf_op jit(solution)/shard_map/while/body/eval_jaxpr/isxy,isbyz->isbxz/dot_general | solution.py:55
  229.4 7.5 %copy.47 = bf16[16,4,2,128,128]{4,1,2,3,0:T(4,128)(2,1)} copy(bf16[16,4,2,128,128]{3,4,2,1,0:T(8,128)(2,1)} %fusion.36) | data formatting | bytes 8388608 | tf_op jit(solution)/shard_map/while/body/eval_jaxpr/convert_element_type | solution.py:58
  236.9 4.5 %convolution_bitcast_fusion.4 = f32[16,8,128,128,1]{3,1,2,0,4:T(8,128)S(1)} fusion(bf16[16,4,2,128,128]{4,1,2,3,0:T(4,128)(2,1)} %copy.47, bf16[32,4,2,8]{3,1,2,0:T(4,128)(2,1)S(1)} %get-tuple-element.305, s32[]{:T(128)S(6)} %select_n.56), kind=kOutput, calls=%fused_computation.6.clone.1 | convolution fusion | flops 33554432 | bytes 12615684 | tf_op jit(solution)/shard_map/while/body/eval_jaxpr/isbxz,isbj->ijxz/dot_general | solution.py:61
  241.4 11.6 %convolution_bitcast_fusion.5 = f32[16,2,8,128,128]{3,4,1,2,0:T(8,128)} fusion(f32[16,8,128,128,1]{3,1,2,0,4:T(8,128)S(1)} %convolution_bitcast_fusion.4, bf16[32,2,128,128]{3,2,1,0:T(8,128)(2,1)} %get-tuple-element.310, s32[]{:T(128)S(6)} %select_n.56), kind=kOutput, calls=%fused_computation.2.clone.1 | convolution fusion | flops 6442450944 | bytes 26214404 | tf_op jit(solution)/shard_map/while/body/eval_jaxpr/iayx,ijyz->iajxz/dot_general | solution.py:64
  253.0 17.5 %copy.48 = f32[16,2,8,128,128]{4,0,1,3,2:T(8,128)} copy(f32[16,2,8,128,128]{3,4,1,2,0:T(8,128)} %convolution_bitcast_fusion.5) | data formatting | bytes 33554432 | tf_op jit(solution)/shard_map/while/body/eval_jaxpr/iayx,ijyz->iajxz/transpose | solution.py:64
  270.5 12.6 %bitcast_add_fusion.2 = f32[4,8,128,128]{3,0,2,1:T(4,128)S(1)} fusion(f32[4,8,128,128]{3,0,2,1:T(4,128)S(1)} %get-tuple-element.290, f32[16,2,8,128,128]{4,0,1,3,2:T(8,128)} %copy.48, pred[]{:T(512)S(6)} %compare.3, f32[32,2,4]{0,2,1:T(4,128)S(1)} %get-tuple-element.304, s32[]{:T(128)S(6)} %select_n.56), kind=kOutput, calls=%fused_computation.8.clone.1 | convolution fusion | flops 202375168 | bytes 20972548 | tf_op jit(solution)/shard_map/while/body/eval_jaxpr/iajxz,iak->kjxz/dot_general | solution.py:70
  283.1 1.6 copy.27
  (24 shorter events, 0.4 us)
Async XLA Ops:
  6.5 39.2 %all-gather.2.cloned.1.call-start = ((), (), s32[]{:S(2)}) async-start(), calls=%async_computation | async-start | bytes 2621440 | tf_op jit(solution)/shard_map/all_gather | solution.py:26
  7.3 139.4 %all-reduce.3.cloned.1.call-start = ((), (), s32[]{:S(2)}) async-start(), calls=%async_computation.1 | async-start | bytes 8388608 | tf_op jit(solution)/shard_map/psum | solution.py:13
  7.3 42.3 %copy-start.2 = (s32[256,2]{0,1:T(2,128)S(1)}, s32[256,2]{0,1:T(2,128)}, u32[]{:S(2)}) copy-start(s32[256,2]{0,1:T(2,128)} %param.11) | copy-start | bytes 6148
  7.3 42.5 %copy-start.1 = (s32[32,4]{0,1:T(4,128)S(1)}, s32[32,4]{0,1:T(4,128)}, u32[]{:S(2)}) copy-start(s32[32,4]{0,1:T(4,128)} %param.8) | copy-start | bytes 1540
  146.7 4.7 %copy-start = (s32[32,4]{0,1:T(4,128)S(1)}, s32[32,4]{0,1:T(4,128)}, u32[]{:S(2)}) copy-start(s32[32,4]{0,1:T(4,128)} %param.9) | copy-start | bytes 1540
Sparse Core Ops, SparseCore 0:
  9.2 36.4 all-gather.1
  49.8 96.8 all-reduce.2
where the time goes:
time: 294 us; the launch traced here: 292 us
  waiting for transfers between devices  134 us (46%)
  matrix products  70.7 us (24%)
  local copies, waits for them, and re-layouts  63.9 us (22%)
  between operations  13.5 us (5%)
  other arithmetic  8.81 us (3%)
    psum x1, waiting for transfers between devices, broadcast(): return lax.psum(kept, axis)  95.3 us
    all_gather x1, waiting for transfers between devices, shards(): left_rows = lax.all_gather(prolongator, 'col', axis=0, tiled=True)  38.4 us
    transpose x2, local copies, waits for them, and re-layouts, one_block(): jnp.einsum('iayx,ijyz->iajxz', left_block.astype(jnp.float32), collected,...  34.9 us
    dot_general x2, matrix products, one_block(): jnp.einsum('iajxz,iak->kjxz', projected, left_onehot, precision=lax.Preci...  25.1 us
    dot_general x2, matrix products, one_block(): jnp.einsum('iayx,ijyz->iajxz', left_block.astype(jnp.float32), collected,...  23.3 us
    convert_element_type x2, local copies, waits for them, and re-layouts, one_block(): (product * live_mask[:, :, None, None, None].astype(jnp.float32)).astype(...  15.1 us
    dot_general x2, matrix products, one_block(): jnp.einsum('isxy,isbyz->isbxz', stiff_rows, right_block, preferred_elemen...  13.4 us
    gather x2, local copies, waits for them, and re-layouts, one_block(): right_block = right_rows[index_rows]  10.5 us
  transfers between devices with their start and end apart: 2, of which 2 were waited for; matrix products, arithmetic and copies ran while one was open for 1% of the time, Pallas kernels for 0%

commit v1 on v0

v1 whole, which is shorter than its diff:
```python
import functools

import jax
import jax.numpy as jnp
from jax import lax
from jax.experimental import pallas as pl
from jax.experimental.pallas import tpu as pltpu
from jax.sharding import PartitionSpec as P

ACC_BYTES = 17 << 20
VMEM_LIMIT = 56 << 20


def left_kernel(group, col_ref, agg_ref, base_ref, *refs):
    *pieces, stiff_ref, out_ref, acc_ref = refs
    cols_count = out_ref.shape[0]
    slots = stiff_ref.shape[1]
    block = stiff_ref.shape[2]
    first_agg = pl.program_id(0) * group
    acc_ref[...] = jnp.zeros_like(acc_ref)

    for number, piece in enumerate(pieces):

        def one_row(j, carry, number=number, piece=piece):
            row = base_ref[number] + j
            left = jnp.concatenate([piece[j, 0].T, piece[j, 1].T], axis=0)
            for s in range(slots):
                col = col_ref[row * slots + s]
                terms = jnp.dot(left, stiff_ref[row, s], preferred_element_type=jnp.float32)
                for a in range(2):
                    agg = agg_ref[row * 2 + a] - first_agg
                    inside = jnp.logical_and(agg >= 0, agg < group)
                    at_col = jnp.where(inside, col, cols_count)
                    at_agg = jnp.where(inside, agg, 0)
                    acc_ref[at_col, at_agg] += terms[a * block : (a + 1) * block]
            return carry

        lax.fori_loop(0, piece.shape[0], one_row, 0)

    def one_col(k, carry):
        out_ref[k] = acc_ref[k].reshape(group * block, block).astype(jnp.bfloat16)
        return carry

    lax.fori_loop(0, cols_count, one_col, 0)


def left_sums(pieces, bases, stiffness, cols, aggs, cols_count, agg_rows):
    block = stiffness.shape[2]
    group = agg_rows
    while group > 1 and (cols_count + 1) * group * block * block * 4 > ACC_BYTES:
        group //= 2
    once = pl.Buffered(1)
    whole = lambda x: pl.BlockSpec(x.shape, lambda g, *_: (0,) * x.ndim, pipeline_mode=once)
    products = stiffness.shape[0] * stiffness.shape[1] * 2
    return pl.pallas_call(
        functools.partial(left_kernel, group),
        grid_spec=pltpu.PrefetchScalarGridSpec(
            num_scalar_prefetch=3,
            grid=(agg_rows // group,),
            in_specs=[whole(x) for x in (*pieces, stiffness)],
            out_specs=pl.BlockSpec(
                (cols_count, group * block, block), lambda g, *_: (0, g, 0), pipeline_mode=once
            ),
            scratch_shapes=[pltpu.VMEM((cols_count + 1, group, block, block), jnp.float32)],
        ),
        out_shape=jax.ShapeDtypeStruct((cols_count, agg_rows * block, block), jnp.bfloat16),
        compiler_params=pltpu.CompilerParams(vmem_limit_bytes=VMEM_LIMIT),
        cost_estimate=pl.CostEstimate(
            flops=4 * products * block**3, bytes_accessed=16 << 20, transcendentals=0
        ),
        name="left_sums",
    )(cols, aggs, bases, *pieces, stiffness)


def right_kernel(count, first, agg_ref, chunk_ref, *refs):
    sums, pieces = refs[:count], refs[count : 2 * count]
    out_ref = refs[-1]
    aggs, block = out_ref.shape[0], out_ref.shape[2]
    per = pieces[0].shape[0]
    if first:
        out_ref[...] = jnp.zeros_like(out_ref)
    else:
        out_ref[...] = refs[2 * count][...]
    for number in range(count):

        def one_row(j, carry, number=number):
            row = chunk_ref[number] * per + j
            right = jnp.concatenate([pieces[number][j, 0], pieces[number][j, 1]], axis=1)
            terms = jnp.dot(sums[number][j], right, preferred_element_type=jnp.float32)
            for b in range(2):
                agg = agg_ref[row * 2 + b]
                part = terms[:, b * block : (b + 1) * block].reshape(aggs, block, block)
                out_ref[:, agg] += part
            return carry

        lax.fori_loop(0, per, one_row, 0)


def right_sums(sums, pieces, chunks, aggs, before, shape):
    count = len(pieces)
    per, block = pieces[0].shape[0], pieces[0].shape[2]
    once = pl.Buffered(1)
    whole = lambda x: pl.BlockSpec(x.shape, lambda g, *_: (0,) * x.ndim, pipeline_mode=once)
    out = jax.ShapeDtypeStruct(shape, jnp.float32)
    rest = () if before is None else (before,)
    return pl.pallas_call(
        functools.partial(right_kernel, count, before is None),
        grid_spec=pltpu.PrefetchScalarGridSpec(
            num_scalar_prefetch=2,
            grid=(1,),
            in_specs=[
                pl.BlockSpec(
                    (per,) + sums.shape[1:],
                    lambda g, agg, chunk, n=n: (chunk[n], 0, 0),
                    pipeline_mode=once,
                )
                for n in range(count)
            ]
            + [whole(x) for x in (*pieces, *rest)],
            out_specs=whole(out),
        ),
        out_shape=out,
        input_output_aliases={} if before is None else {2 + 2 * count: 0},
        compiler_params=pltpu.CompilerParams(vmem_limit_bytes=VMEM_LIMIT),
        cost_estimate=pl.CostEstimate(
            flops=4 * count * per * sums.shape[1] * block**2,
            bytes_accessed=(4 << 20) + count * (2 << 20),
            transcendentals=0,
        ),
        name="right_sums",
    )(aggs, chunks, *([sums] * count), *pieces, *rest)


def shards(stiffness, stiff_columns, stiff_stored, prolongator, prolong_columns):
    rows_count, block = stiffness.shape[0], stiffness.shape[2]
    per = prolongator.shape[0]
    row_count, col_count = lax.axis_size("row"), lax.axis_size("col")
    ratio = row_count // col_count
    row_pos, col_pos = lax.axis_index("row"), lax.axis_index("col")
    range_pos, member = row_pos // ratio, row_pos % ratio
    agg_rows = rows_count // 8
    agg_cols = ratio * agg_rows
    cols_count = ratio * rows_count
    first_fine = col_pos * cols_count

    def across(x, d):
        return lax.ppermute(x, "col", [(c, c ^ d) for c in range(col_count)])

    def fetch(x, m):
        pairs = [
            ((c * ratio + k) * col_count + (q ^ c ^ m), (q * ratio + k) * col_count + c)
            for q in range(col_count)
            for k in range(ratio)
            for c in range(col_count)
        ]
        return lax.ppermute(x, ("row", "col"), pairs)

    def beside(x, j):
        return lax.ppermute(
            x, "row", [(r, r // ratio * ratio + (r + j) % ratio) for r in range(row_count)]
        )

    right = {}
    own = prolongator
    order = list(range(col_count))
    if col_count == 4:
        order = [0, 3, 1, 2]
    near = [d for d in range(1, col_count) if d & (d - 1) == 0]
    pieces = [(own, 0, 0)] + [(across(own, d), d, 0) for d in near]
    for m in order[: col_count // 2]:
        right[m] = fetch(own, m)
    later, *held = lax.optimization_barrier((own, *[x for x, _, _ in pieces[1:]]))
    pieces[1:] = [(x, d, s) for x, (_, d, s) in zip(held, pieces[1:])]
    half = per // 2
    for d in range(1, col_count):
        if d in near:
            continue
        low = d & -d
        if d & (d - 1) == low or (d ^ low) in near:
            high = d ^ low
            by = {x_d: x for x, x_d, _ in pieces}
            pieces.append((across(by[high][:half], low), d, 0))
            pieces.append((across(by[low][half:], high), d, half))
        else:
            pieces.append((across(later, d), d, 0))
    for m in order[col_count // 2 :]:
        right[m] = fetch(later, m)

    cols = jnp.where(stiff_stored != 0, stiff_columns - first_fine, cols_count).reshape(-1)
    left_aggs = (
        lax.dynamic_slice_in_dim(prolong_columns, row_pos * rows_count, rows_count, 0)
        - row_pos * agg_rows
    ).reshape(-1)
    right_aggs = (
        lax.dynamic_slice_in_dim(prolong_columns, first_fine, cols_count, 0) - col_pos * agg_cols
    ).reshape(-1)
    bases = jnp.stack([(col_pos ^ d) * per + s for _, d, s in pieces]).astype(jnp.int32)

    sums = left_sums(
        [x for x, _, _ in pieces], bases, stiffness, cols, left_aggs, cols_count, agg_rows
    )

    shape = (agg_rows, agg_cols, block, block)
    coarse = None
    for part in (order[: col_count // 2], order[col_count // 2 :]):
        arrays, chunks = [], []
        for m in part:
            for j in range(ratio):
                arrays.append(right[m] if j == 0 else beside(right[m], j))
                panel = (member - j) % ratio
                chunks.append(panel * col_count + (range_pos ^ col_pos ^ m))
        chunks = jnp.stack(chunks).astype(jnp.int32)
        coarse = right_sums(sums, arrays, chunks, right_aggs, coarse, shape)
    return coarse


def solution(mesh):
    return jax.shard_map(
        shards,
        mesh=mesh,
        in_specs=(
            P("row", "col", None, None),
            P("row", "col"),
            P("row", "col"),
            P(("row", "col"), None, None, None),
            P(),
        ),
        out_specs=P("row", "col", None, None),
        check_vma=False,
    )
```

time: 294 us -> 106 us (0.36)
  waiting for transfers between devices: 134 us -> 16.8 us
  matrix products: 70.7 us -> 0 us
  local copies, waits for them, and re-layouts: 63.9 us -> 5.99 us
  Pallas kernels: 0 us -> 42.7 us
  starting transfers between devices: 0.04 us -> 36.5 us
  between operations: 13.5 us -> 0.1 us
  other arithmetic: 8.81 us -> 3.4 us
    psum x1 -> x0, waiting for transfers between devices: 95.3 us -> none  [broadcast(): return lax.psum(kept, axis)]
    dot_general x8 -> x0, matrix products: 70.7 us -> none  [the longest x2 25.1 us: one_block(): jnp.einsum('iajxz,iak->kjxz', projected, left_onehot, precision=lax.Preci...]
    pallas_call x0 -> x3, Pallas kernels: none -> 42.7 us  [the longest x2 25.1 us: right_sums(): pl.pallas_call(functools.partial(right_kernel, count, before is None), gr...]
    all_gather x1 -> x0, waiting for transfers between devices: 38.4 us -> none  [shards(): left_rows = lax.all_gather(prolongator, 'col', axis=0, tiled=True)]
    ppermute x0 -> x12, starting transfers between devices: none -> 36.5 us  [the longest x4 23.1 us: fetch(): return lax.ppermute(x, ('row', 'col'), pairs)]
    transpose x2 -> x0, local copies, waits for them, and re-layouts: 34.9 us -> none  [one_block(): jnp.einsum('iayx,ijyz->iajxz', left_block.astype(jnp.float32), collected,...]
    ppermute x0 -> x12, waiting for transfers between devices: none -> 16.8 us  [the longest x4 8.9 us: fetch(): return lax.ppermute(x, ('row', 'col'), pairs)]
    convert_element_type x2 -> x0, local copies, waits for them, and re-layouts: 15.1 us -> none  [one_block(): (product * live_mask[:, :, None, None, None].astype(jnp.float32)).astype(...]
  transfers between devices with their start and end apart: 2 -> 12, of which waited for: 2 -> 5; matrix products, arithmetic and copies ran while one was open for 1% -> 7% of each run, Pallas kernels for 0% -> 28%
where the time goes in v1:
time: 106 us
  Pallas kernels  42.7 us (40%)
  starting transfers between devices  36.5 us (34%)
  waiting for transfers between devices  16.8 us (16%)
  local copies, waits for them, and re-layouts  5.99 us (6%)
  other arithmetic  3.4 us (3%)
    pallas_call x2, Pallas kernels, right_sums(): pl.pallas_call(functools.partial(right_kernel, count, before is None), gr...  25.1 us
    ppermute x4, starting transfers between devices, fetch(): return lax.ppermute(x, ('row', 'col'), pairs)  23.1 us
    pallas_call x1, Pallas kernels, left_sums(): pl.pallas_call(functools.partial(left_kernel, group), grid_spec=pltpu.Pre...  17.6 us
    ppermute x4, starting transfers between devices, beside(): lax.ppermute(x, 'row', [(r, r // ratio * ratio + (r + j) % ratio) for r i...  9.39 us
    ppermute x4, waiting for transfers between devices, fetch(): return lax.ppermute(x, ('row', 'col'), pairs)  8.9 us
    ppermute x4, waiting for transfers between devices, across(): return lax.ppermute(x, 'col', [(c, c ^ d) for c in range(col_count)])  7.88 us
    ppermute x4, starting transfers between devices, across(): return lax.ppermute(x, 'col', [(c, c ^ d) for c in range(col_count)])  4.06 us
  transfers between devices with their start and end apart: 12, of which 5 were waited for; matrix products, arithmetic and copies ran while one was open for 7% of the time, Pallas kernels for 28%

profile of v1, /device:TPU:5, one launch (start us, length us, event | category | flops | bytes accessed | tf_op | source)
XLA Modules:
  0.0 105.5 jit_solution(5405348075711537802)
XLA Ops:
  0.0 1.2 %collective-permute-start = (bf16[8,2,128,128]{3,2,1,0:T(8,128)(2,1)}, bf16[8,2,128,128]{3,2,1,0:T(8,128)(2,1)S(1)}, u32[]{:S(2)}, u32[]{:S(2)}) collective-permute-start(bf16[8,2,128,128]{3,2,1,0:T(8,128)(2,1)} %refs_0_.1), channel_id=1, source_target_pairs={{0,1},{1,0},{2,3},{3,2},{4,5},{5,4},{6,7},{7,6},{8,9},{9,8},{10,11... | collective-permute-start | bytes 1572872 | tf_op jit(solution)/shard_map/ppermute | solution.py:147
  1.2 0.2 collective-permute-start.1
  1.4 4.2 %collective-permute-start.10 = (bf16[8,2,128,128]{3,2,1,0:T(8,128)(2,1)}, bf16[8,2,128,128]{3,2,1,0:T(8,128)(2,1)S(1)}, u32[]{:S(2)}, u32[]{:S(2)}) collective-permute-start(bf16[8,2,128,128]{3,2,1,0:T(8,128)(2,1)} %refs_0_.1), channel_id=1, source_target_pairs={{3,0},{10,1},{17,2},{24,3},{7,4},{14,5},{21,6},{28,7},{2,8},{11,9}... | collective-permute-start | bytes 1572872 | tf_op jit(solution)/shard_map/ppermute | solution.py:156
  5.6 3.0 %collective-permute-start.8 = (bf16[8,2,128,128]{3,2,1,0:T(8,128)(2,1)}, bf16[8,2,128,128]{3,2,1,0:T(8,128)(2,1)S(1)}, u32[]{:S(2)}, u32[]{:S(2)}) collective-permute-start(bf16[8,2,128,128]{3,2,1,0:T(8,128)(2,1)} %refs_0_.1), channel_id=1, source_target_pairs={{0,0},{9,1},{18,2},{27,3},{4,4},{13,5},{22,6},{31,7},{1,8},{8,9},{... | collective-permute-start | bytes 1572872 | tf_op jit(solution)/shard_map/ppermute | solution.py:156
  8.6 7.7 %collective-permute-done.refs_1_ = bf16[8,2,128,128]{3,2,1,0:T(8,128)(2,1)S(1)} collective-permute-done((bf16[8,2,128,128]{3,2,1,0:T(8,128)(2,1)}, bf16[8,2,128,128]{3,2,1,0:T(8,128)(2,1)S(1)}, u32[]{:S(2)}, u32[]{:S(2)}) %collective-permute-start) | collective-permute-done | bytes 524320 | tf_op jit(solution)/shard_map/ppermute | solution.py:147
  16.3 14.0 %collective-permute-start.4 = (bf16[8,2,128,128]{3,2,1,0:T(8,128)(2,1)}, bf16[8,2,128,128]{3,2,1,0:T(8,128)(2,1)S(1)}, u32[]{:S(2)}, u32[]{:S(2)}) collective-permute-start(bf16[8,2,128,128]{3,2,1,0:T(8,128)(2,1)} %refs_0_.1), channel_id=1, source_target_pairs={{1,0},{8,1},{19,2},{26,3},{5,4},{12,5},{23,6},{30,7},{0,8},{9,9},{... | collective-permute-start | bytes 1572872 | tf_op jit(solution)/shard_map/ppermute | solution.py:156
  30.3 1.9 %collective-permute-start.6 = (bf16[8,2,128,128]{3,2,1,0:T(8,128)(2,1)}, bf16[8,2,128,128]{3,2,1,0:T(8,128)(2,1)S(1)}, u32[]{:S(2)}, u32[]{:S(2)}) collective-permute-start(bf16[8,2,128,128]{3,2,1,0:T(8,128)(2,1)} %refs_0_.1), channel_id=1, source_target_pairs={{2,0},{11,1},{16,2},{25,3},{6,4},{15,5},{20,6},{29,7},{3,8},{10,9}... | collective-permute-start | bytes 1572872 | tf_op jit(solution)/shard_map/ppermute | solution.py:156
  32.2 0.7 slice.6
  33.0 0.8 dynamic-slice_subtract_fusion
  33.7 0.7 subtract_select_fusion
  34.4 0.7 slice.7
  35.1 2.6 %collective-permute-start.3 = (bf16[4,2,128,128]{3,2,1,0:T(8,128)(2,1)}, bf16[4,2,128,128]{3,2,1,0:T(8,128)(2,1)}, u32[]{:S(2)}, u32[]{:S(2)}) collective-permute-start(bf16[4,2,128,128]{3,2,1,0:T(8,128)(2,1)} %slice.7), channel_id=1, source_target_pairs={{0,2},{1,3},{2,0},{3,1},{4,6},{5,7},{6,4},{7,5},{8,10},{9,11},{10,... | collective-permute-start | bytes 786440 | tf_op jit(solution)/shard_map/ppermute | solution.py:147
  37.8 5.3 %collective-permute-done.8.refs_4_ = bf16[8,2,128,128]{3,2,1,0:T(8,128)(2,1)S(1)} collective-permute-done((bf16[8,2,128,128]{3,2,1,0:T(8,128)(2,1)}, bf16[8,2,128,128]{3,2,1,0:T(8,128)(2,1)S(1)}, u32[]{:S(2)}, u32[]{:S(2)}) %collective-permute-start.8) | collective-permute-done | bytes 524320 | tf_op jit(solution)/shard_map/ppermute | solution.py:156
  43.1 4.4 %collective-permute-start.11 = (bf16[8,2,128,128]{3,2,1,0:T(8,128)(2,1)S(1)}, bf16[8,2,128,128]{3,2,1,0:T(8,128)(2,1)}, u32[]{:S(2)}, u32[]{:S(2)}) collective-permute-start(bf16[8,2,128,128]{3,2,1,0:T(8,128)(2,1)S(1)} %collective-permute-done.10.refs_6_), channel_id=1, source_target_pairs={{0,4},{4,0},{8,12},{12,8},{16,20},{20,16},{24,28},{28,24},{1,5},{5... | collective-permute-start | bytes 1572872 | tf_op jit(solution)/shard_map/ppermute | solution.py:159
  47.5 0.2 collective-permute-done.2.refs_3_
  47.7 0.5 collective-permute-start.9
  48.1 0.8 dynamic-slice_subtract_fusion.1
  49.0 0.6 reshape.11.agg_ref
  49.7 0.6 reshape.10.col_ref
  50.4 0.7 reshape.9.agg_ref
  51.1 0.7 stack.58.base_ref
  51.8 3.2 %collective-permute-done.4.refs_4_ = bf16[8,2,128,128]{3,2,1,0:T(8,128)(2,1)S(1)} collective-permute-done((bf16[8,2,128,128]{3,2,1,0:T(8,128)(2,1)}, bf16[8,2,128,128]{3,2,1,0:T(8,128)(2,1)S(1)}, u32[]{:S(2)}, u32[]{:S(2)}) %collective-permute-start.4) | collective-permute-done | bytes 524320 | tf_op jit(solution)/shard_map/ppermute | solution.py:156
  55.0 1.5 %collective-permute-start.5 = (bf16[8,2,128,128]{3,2,1,0:T(8,128)(2,1)S(1)}, bf16[8,2,128,128]{3,2,1,0:T(8,128)(2,1)S(1)}, u32[]{:S(2)}, u32[]{:S(2)}) collective-permute-start(bf16[8,2,128,128]{3,2,1,0:T(8,128)(2,1)S(1)} %collective-permute-done.4.refs_4_), channel_id=1, source_target_pairs={{0,4},{4,0},{8,12},{12,8},{16,20},{20,16},{24,28},{28,24},{1,5},{5... | collective-permute-start | bytes 1572872 | tf_op jit(solution)/shard_map/ppermute | solution.py:159
  56.5 0.3 collective-permute-done.6.refs_6_
  56.9 3.0 %collective-permute-start.7 = (bf16[8,2,128,128]{3,2,1,0:T(8,128)(2,1)S(1)}, bf16[8,2,128,128]{3,2,1,0:T(8,128)(2,1)S(1)}, u32[]{:S(2)}, u32[]{:S(2)}) collective-permute-start(bf16[8,2,128,128]{3,2,1,0:T(8,128)(2,1)S(1)} %collective-permute-done.6.refs_6_), channel_id=1, source_target_pairs={{0,4},{4,0},{8,12},{12,8},{16,20},{20,16},{24,28},{28,24},{1,5},{5... | collective-permute-start | bytes 1572872 | tf_op jit(solution)/shard_map/ppermute | solution.py:159
  59.9 0.6 pad_add_fusion.1.chunk_ref
  60.5 0.6 pad_add_fusion.chunk_ref
  61.1 17.6 %left_sums.1.refs_0_.refs_1_.refs_2_.refs_3_ = bf16[64,512,128]{2,1,0:T(8,128)(2,1)} custom-call(s32[128]{0:T(128)} %reshape.10.col_ref, s32[64]{0:T(128)} %reshape.11.agg_ref, s32[5]{0:T(128)} %stack.58.base_ref, bf16[8,2,128,128]{3,2,1,0:T(8,128)(2,1)} %refs_0_.1, bf16[8,2,128,128]{3,2,1,0:T(8,128)(2,1)} %copy-done, bf16[8,2,128,128]{3,2,1,0:T(8,128)(2,1)} %copy-done.1, ...), custom_call_target="tpu_custom_call" | custom-call | flops 2147483648 | bytes 16777216 | tf_op jit(solution)/shard_map/left_sums/pallas_call | solution.py:55
  78.8 12.2 %right_sums.2.refs_8_ = f32[4,8,128,128]{3,2,1,0:T(8,128)} custom-call(s32[128]{0:T(128)} %reshape.9.agg_ref, s32[4]{0:T(128)} %pad_add_fusion.1.chunk_ref, bf16[64,512,128]{2,1,0:T(8,128)(2,1)} %left_sums.1.refs_0_.refs_1_.refs_2_.refs_3_, bf16[64,512,128]{2,1,0:T(8,128)(2,1)} %left_sums.1.refs_0_.refs_1_.refs_2_.refs_3_, ...), custom_call_target="tpu_custom_call" | custom-call | flops 1073741824 | bytes 12582912 | tf_op jit(solution)/shard_map/right_sums/pallas_call | solution.py:106
  90.9 0.9 copy-done.6
  91.8 0.8 copy-done.7
  92.6 12.9 %right_sums.3 = f32[4,8,128,128]{3,2,1,0:T(8,128)} custom-call(s32[128]{0:T(128)} %reshape.9.agg_ref, s32[4]{0:T(128)} %pad_add_fusion.chunk_ref, bf16[64,512,128]{2,1,0:T(8,128)(2,1)} %left_sums.1.refs_0_.refs_1_.refs_2_.refs_3_, bf16[64,512,128]{2,1,0:T(8,128)(2,1)} %left_sums.1.refs_0_.refs_1_.refs_2_.refs_3_, ...), custom_call_target="tpu_custom_call", output_to_operand_aliasing={{}: (10, {})} | custom-call | flops 1073741824 | bytes 12582912 | tf_op jit(solution)/shard_map/right_sums/pallas_call | solution.py:106
  (27 shorter events, 0.3 us)
Async XLA Ops:
  0.0 16.3 %collective-permute-start = (bf16[8,2,128,128]{3,2,1,0:T(8,128)(2,1)}, bf16[8,2,128,128]{3,2,1,0:T(8,128)(2,1)S(1)}, u32[]{:S(2)}, u32[]{:S(2)}) collective-permute-start(bf16[8,2,128,128]{3,2,1,0:T(8,128)(2,1)} %refs_0_.1), channel_id=1, source_target_pairs={{0,1},{1,0},{2,3},{3,2},{4,5},{5,4},{6,7},{7,6},{8,9},{9,8},{10,11... | collective-permute-start | bytes 1572872 | tf_op jit(solution)/shard_map/ppermute | solution.py:147
  1.2 15.1 %collective-permute-start.1 = (bf16[8,2,128,128]{3,2,1,0:T(8,128)(2,1)}, bf16[8,2,128,128]{3,2,1,0:T(8,128)(2,1)S(1)}, u32[]{:S(2)}, u32[]{:S(2)}) collective-permute-start(bf16[8,2,128,128]{3,2,1,0:T(8,128)(2,1)} %refs_0_.1), channel_id=1, source_target_pairs={{0,2},{1,3},{2,0},{3,1},{4,6},{5,7},{6,4},{7,5},{8,10},{9,11},{10,... | collective-permute-start | bytes 1572872 | tf_op jit(solution)/shard_map/ppermute | solution.py:147
  1.4 33.7 %collective-permute-start.10 = (bf16[8,2,128,128]{3,2,1,0:T(8,128)(2,1)}, bf16[8,2,128,128]{3,2,1,0:T(8,128)(2,1)S(1)}, u32[]{:S(2)}, u32[]{:S(2)}) collective-permute-start(bf16[8,2,128,128]{3,2,1,0:T(8,128)(2,1)} %refs_0_.1), channel_id=1, source_target_pairs={{3,0},{10,1},{17,2},{24,3},{7,4},{14,5},{21,6},{28,7},{2,8},{11,9}... | collective-permute-start | bytes 1572872 | tf_op jit(solution)/shard_map/ppermute | solution.py:156
  5.6 37.5 %collective-permute-start.8 = (bf16[8,2,128,128]{3,2,1,0:T(8,128)(2,1)}, bf16[8,2,128,128]{3,2,1,0:T(8,128)(2,1)S(1)}, u32[]{:S(2)}, u32[]{:S(2)}) collective-permute-start(bf16[8,2,128,128]{3,2,1,0:T(8,128)(2,1)} %refs_0_.1), channel_id=1, source_target_pairs={{0,0},{9,1},{18,2},{27,3},{4,4},{13,5},{22,6},{31,7},{1,8},{8,9},{... | collective-permute-start | bytes 1572872 | tf_op jit(solution)/shard_map/ppermute | solution.py:156
  16.3 44.8 %copy-start = (bf16[8,2,128,128]{3,2,1,0:T(8,128)(2,1)}, bf16[8,2,128,128]{3,2,1,0:T(8,128)(2,1)S(1)}, u32[]{:S(2)}) copy-start(bf16[8,2,128,128]{3,2,1,0:T(8,128)(2,1)S(1)} %collective-permute-done.refs_1_) | copy-start | bytes 1572868
  16.3 44.8 %copy-start.1 = (bf16[8,2,128,128]{3,2,1,0:T(8,128)(2,1)}, bf16[8,2,128,128]{3,2,1,0:T(8,128)(2,1)S(1)}, u32[]{:S(2)}) copy-start(bf16[8,2,128,128]{3,2,1,0:T(8,128)(2,1)S(1)} %collective-permute-done.1.refs_2_) | copy-start | bytes 1572868
  16.3 38.7 %collective-permute-start.4 = (bf16[8,2,128,128]{3,2,1,0:T(8,128)(2,1)}, bf16[8,2,128,128]{3,2,1,0:T(8,128)(2,1)S(1)}, u32[]{:S(2)}, u32[]{:S(2)}) collective-permute-start(bf16[8,2,128,128]{3,2,1,0:T(8,128)(2,1)} %refs_0_.1), channel_id=1, source_target_pairs={{1,0},{8,1},{19,2},{26,3},{5,4},{12,5},{23,6},{30,7},{0,8},{9,9},{... | collective-permute-start | bytes 1572872 | tf_op jit(solution)/shard_map/ppermute | solution.py:156
  30.3 26.5 %collective-permute-start.6 = (bf16[8,2,128,128]{3,2,1,0:T(8,128)(2,1)}, bf16[8,2,128,128]{3,2,1,0:T(8,128)(2,1)S(1)}, u32[]{:S(2)}, u32[]{:S(2)}) collective-permute-start(bf16[8,2,128,128]{3,2,1,0:T(8,128)(2,1)} %refs_0_.1), channel_id=1, source_target_pairs={{2,0},{11,1},{16,2},{25,3},{6,4},{15,5},{20,6},{29,7},{3,8},{10,9}... | collective-permute-start | bytes 1572872 | tf_op jit(solution)/shard_map/ppermute | solution.py:156
  33.0 14.7 %collective-permute-start.2 = (bf16[4,2,128,128]{3,2,1,0:T(8,128)(2,1)}, bf16[4,2,128,128]{3,2,1,0:T(8,128)(2,1)S(1)}, u32[]{:S(2)}, u32[]{:S(2)}) collective-permute-start(bf16[4,2,128,128]{3,2,1,0:T(8,128)(2,1)} %slice.6), channel_id=1, source_target_pairs={{0,1},{1,0},{2,3},{3,2},{4,5},{5,4},{6,7},{7,6},{8,9},{9,8},{10,11... | collective-permute-start | bytes 786440 | tf_op jit(solution)/shard_map/ppermute | solution.py:147
  35.1 43.6 %copy-start.2 = (bf16[8,2,128,128]{3,2,1,0:T(8,128)(2,1)}, bf16[8,2,128,128]{3,2,1,0:T(8,128)(2,1)S(1)}, u32[]{:S(2)}) copy-start(bf16[8,2,128,128]{3,2,1,0:T(8,128)(2,1)S(1)} %collective-permute-done.10.refs_6_) | copy-start | bytes 1572868
  35.1 25.9 %collective-permute-start.3 = (bf16[4,2,128,128]{3,2,1,0:T(8,128)(2,1)}, bf16[4,2,128,128]{3,2,1,0:T(8,128)(2,1)}, u32[]{:S(2)}, u32[]{:S(2)}) collective-permute-start(bf16[4,2,128,128]{3,2,1,0:T(8,128)(2,1)} %slice.7), channel_id=1, source_target_pairs={{0,2},{1,3},{2,0},{3,1},{4,6},{5,7},{6,4},{7,5},{8,10},{9,11},{10,... | collective-permute-start | bytes 786440 | tf_op jit(solution)/shard_map/ppermute | solution.py:147
  43.1 35.7 %copy-start.4 = (bf16[8,2,128,128]{3,2,1,0:T(8,128)(2,1)}, bf16[8,2,128,128]{3,2,1,0:T(8,128)(2,1)S(1)}, u32[]{:S(2)}) copy-start(bf16[8,2,128,128]{3,2,1,0:T(8,128)(2,1)S(1)} %collective-permute-done.8.refs_4_) | copy-start | bytes 1572868
  43.1 35.7 %collective-permute-start.11 = (bf16[8,2,128,128]{3,2,1,0:T(8,128)(2,1)S(1)}, bf16[8,2,128,128]{3,2,1,0:T(8,128)(2,1)}, u32[]{:S(2)}, u32[]{:S(2)}) collective-permute-start(bf16[8,2,128,128]{3,2,1,0:T(8,128)(2,1)S(1)} %collective-permute-done.10.refs_6_), channel_id=1, source_target_pairs={{0,4},{4,0},{8,12},{12,8},{16,20},{20,16},{24,28},{28,24},{1,5},{5... | collective-permute-start | bytes 1572872 | tf_op jit(solution)/shard_map/ppermute | solution.py:159
  47.7 13.4 %copy-start.8 = (bf16[4,2,128,128]{3,2,1,0:T(8,128)(2,1)}, bf16[4,2,128,128]{3,2,1,0:T(8,128)(2,1)S(1)}, u32[]{:S(2)}) copy-start(bf16[4,2,128,128]{3,2,1,0:T(8,128)(2,1)S(1)} %collective-permute-done.2.refs_3_) | copy-start | bytes 786436
  47.7 31.1 %collective-permute-start.9 = (bf16[8,2,128,128]{3,2,1,0:T(8,128)(2,1)S(1)}, bf16[8,2,128,128]{3,2,1,0:T(8,128)(2,1)}, u32[]{:S(2)}, u32[]{:S(2)}) collective-permute-start(bf16[8,2,128,128]{3,2,1,0:T(8,128)(2,1)S(1)} %collective-permute-done.8.refs_4_), channel_id=1, source_target_pairs={{0,4},{4,0},{8,12},{12,8},{16,20},{20,16},{24,28},{28,24},{1,5},{5... | collective-permute-start | bytes 1572872 | tf_op jit(solution)/shard_map/ppermute | solution.py:159
  55.0 23.7 %copy-start.3 = (bf16[8,2,128,128]{3,2,1,0:T(8,128)(2,1)}, bf16[8,2,128,128]{3,2,1,0:T(8,128)(2,1)S(1)}, u32[]{:S(2)}) copy-start(bf16[8,2,128,128]{3,2,1,0:T(8,128)(2,1)S(1)} %collective-permute-done.4.refs_4_) | copy-start | bytes 1572868
  55.0 35.9 %collective-permute-start.5 = (bf16[8,2,128,128]{3,2,1,0:T(8,128)(2,1)S(1)}, bf16[8,2,128,128]{3,2,1,0:T(8,128)(2,1)S(1)}, u32[]{:S(2)}, u32[]{:S(2)}) collective-permute-start(bf16[8,2,128,128]{3,2,1,0:T(8,128)(2,1)S(1)} %collective-permute-done.4.refs_4_), channel_id=1, source_target_pairs={{0,4},{4,0},{8,12},{12,8},{16,20},{20,16},{24,28},{28,24},{1,5},{5... | collective-permute-start | bytes 1572872 | tf_op jit(solution)/shard_map/ppermute | solution.py:159
  56.9 21.9 %copy-start.5 = (bf16[8,2,128,128]{3,2,1,0:T(8,128)(2,1)}, bf16[8,2,128,128]{3,2,1,0:T(8,128)(2,1)S(1)}, u32[]{:S(2)}) copy-start(bf16[8,2,128,128]{3,2,1,0:T(8,128)(2,1)S(1)} %collective-permute-done.6.refs_6_) | copy-start | bytes 1572868
  56.9 34.1 %collective-permute-start.7 = (bf16[8,2,128,128]{3,2,1,0:T(8,128)(2,1)S(1)}, bf16[8,2,128,128]{3,2,1,0:T(8,128)(2,1)S(1)}, u32[]{:S(2)}, u32[]{:S(2)}) collective-permute-start(bf16[8,2,128,128]{3,2,1,0:T(8,128)(2,1)S(1)} %collective-permute-done.6.refs_6_), channel_id=1, source_target_pairs={{0,4},{4,0},{8,12},{12,8},{16,20},{20,16},{24,28},{28,24},{1,5},{5... | collective-permute-start | bytes 1572872 | tf_op jit(solution)/shard_map/ppermute | solution.py:159
  90.9 0.9 copy-start.6
  91.8 0.8 copy-start.7

commit v2 on v0

v2 whole, which is shorter than its diff:
```python
import functools

import jax
import jax.numpy as jnp
from jax import lax
from jax.experimental import pallas as pl
from jax.experimental.pallas import tpu as pltpu
from jax.sharding import PartitionSpec as P

G = 8
UNIT = 8
VMEM_LIMIT = 16 << 20
HBM = pl.BlockSpec(memory_space=pltpu.HBM)
SMEM = pl.BlockSpec(memory_space=pltpu.SMEM)
VMEM = pl.BlockSpec(memory_space=pltpu.VMEM)
ROW_BITS, AGG_BITS = 8, 5


def in_vmem(x):
    return pltpu.with_memory_space_constraint(x, pltpu.VMEM)


def in_hbm(x):
    return pltpu.with_memory_space_constraint(x, pltpu.HBM)


class Sizes:
    def __init__(self, stiffness, prolongator, row_count, col_count):
        self.rows, self.slots, self.block = stiffness.shape[:3]
        self.per = prolongator.shape[0]
        self.row_count, self.col_count = row_count, col_count
        self.ratio = row_count // col_count
        self.agg_rows = self.rows // G
        self.agg_cols = self.ratio * self.agg_rows
        self.cols = self.ratio * self.rows
        self.chunks = self.cols // self.per
        self.slots_count = self.rows * self.slots
        order = [0, 3, 1, 2] if col_count == 4 else list(range(col_count))
        self.early, self.late = order[: col_count // 2], order[col_count // 2 :]
        members = range(self.ratio)
        self.batches = [
            [(m, j) for m in self.early for j in members],
            [(m, 0) for m in self.late],
            [(m, j) for m in self.late for j in members if j],
        ]
        spare = len(self.batches) * (UNIT - 1)
        self.units = -(-(self.slots_count + spare) // UNIT)
        self.entries = self.units * UNIT
        self.place_at = 0
        self.start_at = self.slots_count
        self.entry_at = self.start_at + len(self.batches) + 1
        self.table = self.entry_at + self.entries
        self.per_bits = self.per.bit_length() - 1
        assert self.per == 1 << self.per_bits
        assert self.chunks * self.per <= 1 << ROW_BITS
        assert max(self.agg_rows, self.agg_cols) < 1 << AGG_BITS
        block = self.block
        self.terms_shape = (self.entries + 1, 2 * block, block)
        self.acc_shape = ((self.agg_rows + 1) * self.agg_cols, block, block)


def position(z):
    row_pos, col_pos = lax.axis_index("row"), lax.axis_index("col")
    return row_pos, col_pos, row_pos // z.ratio, row_pos % z.ratio


def list_slots(z, columns_ref, stored_ref, prolong_ref, table_ref, fill_ref, batch_ref, base_ref):
    row_pos, col_pos, range_pos, member = position(z)
    first_fine = col_pos * z.cols
    first_row = row_pos * z.rows
    first_agg = row_pos * z.agg_rows
    first_agg_col = col_pos * z.agg_cols
    right_shift = ROW_BITS + 2 * AGG_BITS
    padding = z.agg_rows * ((1 << ROW_BITS) + (1 << (ROW_BITS + AGG_BITS)))

    for b, batch in enumerate(z.batches):
        fill_ref[b] = 0
        for at, (m, j) in enumerate(batch):
            panel = lax.rem(member - j + z.ratio, z.ratio)
            chunk = panel * z.col_count + (range_pos ^ col_pos ^ m)
            batch_ref[chunk] = b
            base_ref[chunk] = at * z.per

    def count(i, carry):
        for s in range(z.slots):
            chunk = lax.shift_right_logical(columns_ref[s, i] - first_fine, z.per_bits)
            b = batch_ref[chunk]
            fill_ref[b] += jnp.where(stored_ref[s, i] != 0, 1, 0)
        return carry

    lax.fori_loop(0, z.rows, count, 0)

    at = 0
    for b in range(len(z.batches)):
        table_ref[z.start_at + b] = at
        after = at + (fill_ref[b] + (UNIT - 1)) // UNIT * UNIT
        fill_ref[b] = at

        @pl.when(after > at)
        def _(after=after):
            for u in range(1, UNIT):
                table_ref[z.entry_at + after - u] = padding

        at = after
    table_ref[z.start_at + len(z.batches)] = at

    def place(i, carry):
        first = prolong_ref[0, first_row + i] - first_agg
        second = prolong_ref[1, first_row + i] - first_agg
        left = first * (1 << ROW_BITS) + second * (1 << (ROW_BITS + AGG_BITS))
        for s in range(z.slots):
            column = columns_ref[s, i]
            col = column - first_fine
            chunk = lax.shift_right_logical(col, z.per_bits)
            b = batch_ref[chunk]
            row = base_ref[chunk] + (col & (z.per - 1))
            right = (prolong_ref[0, column] - first_agg_col) * (1 << right_shift)
            right += (prolong_ref[1, column] - first_agg_col) * (1 << (right_shift + AGG_BITS))
            stored = stored_ref[s, i] != 0
            at = fill_ref[b]
            table_ref[z.place_at + i * z.slots + s] = jnp.where(stored, at, z.entries)

            @pl.when(stored)
            def _(b=b, at=at, entry=row + left + right):
                table_ref[z.entry_at + at] = entry
                fill_ref[b] = at + 1

        return carry

    lax.fori_loop(0, z.rows, place, 0)


def left_rows(z, chunk, parts, table_ref, stiff_ref, terms_ref):
    first = chunk * z.per
    row = 0
    for piece in parts:
        for j in range(piece.shape[0]):
            left = jnp.concatenate([piece[j, 0].T, piece[j, 1].T], axis=0)
            for s in range(0, z.slots, 2):
                pair = range(s, min(s + 2, z.slots))
                right = jnp.concatenate([stiff_ref[first + row, t] for t in pair], axis=1)
                terms = jnp.dot(left, right, preferred_element_type=jnp.float32)
                for at, t in enumerate(pair):
                    place = table_ref[z.place_at + (first + row) * z.slots + t]
                    terms_ref[place] = terms[:, at * z.block : (at + 1) * z.block].astype(
                        jnp.bfloat16
                    )
            row += 1


def first_kernel(z, columns_ref, stored_ref, prolong_ref, stiff_ref, own_ref, *refs):
    table_ref, held_ref, terms_ref, acc_ref, *scratch, sem = refs
    col_pos = lax.axis_index("col")
    load = pltpu.make_async_copy(stiff_ref, held_ref, sem)
    load.start()
    list_slots(z, columns_ref, stored_ref, prolong_ref, table_ref, *scratch)
    acc_ref[...] = jnp.zeros_like(acc_ref)
    load.wait()
    left_rows(z, col_pos, [own_ref], table_ref, held_ref, terms_ref)


def first_step(z, columns, stored, prolong_columns, stiffness, own):
    return pl.pallas_call(
        functools.partial(first_kernel, z),
        in_specs=[SMEM] * 3 + [HBM, VMEM],
        out_specs=[SMEM, VMEM, VMEM, VMEM],
        out_shape=[
            jax.ShapeDtypeStruct((z.table,), jnp.int32),
            pltpu.VMEM(stiffness.shape, stiffness.dtype),
            pltpu.VMEM(z.terms_shape, jnp.bfloat16),
            pltpu.VMEM(z.acc_shape, jnp.float32),
        ],
        scratch_shapes=[
            pltpu.SMEM((len(z.batches),), jnp.int32),
            pltpu.SMEM((z.chunks,), jnp.int32),
            pltpu.SMEM((z.chunks,), jnp.int32),
            pltpu.SemaphoreType.DMA,
        ],
        compiler_params=pltpu.CompilerParams(vmem_limit_bytes=VMEM_LIMIT),
        cost_estimate=pl.CostEstimate(
            flops=1 << 33, bytes_accessed=64 << 20, transcendentals=0
        ),
        name="first_step",
    )(columns.T, stored.T, prolong_columns.T, in_hbm(stiffness), own)


def left_kernel(z, groups, table_ref, held_ref, *refs):
    terms_ref = refs[-1]
    col_pos = lax.axis_index("col")
    taken = 0
    for d, count in groups:
        left_rows(z, col_pos ^ d, refs[taken : taken + count], table_ref, held_ref, terms_ref)
        taken += count


def left_terms(z, groups, table, held, terms):
    pieces = [x for _, parts in groups for x in parts]
    n = len(groups)
    return pl.pallas_call(
        functools.partial(left_kernel, z, [(d, len(parts)) for d, parts in groups]),
        in_specs=[SMEM, VMEM] + [VMEM] * len(pieces) + [VMEM],
        out_specs=VMEM,
        out_shape=pltpu.VMEM(z.terms_shape, jnp.bfloat16),
        input_output_aliases={2 + len(pieces): 0},
        compiler_params=pltpu.CompilerParams(vmem_limit_bytes=VMEM_LIMIT),
        cost_estimate=pl.CostEstimate(
            flops=n << 32, bytes_accessed=n * (32 << 20), transcendentals=0
        ),
        name="left_terms",
    )(table, in_vmem(held), *pieces, in_vmem(terms))


def right_kernel(z, number, last, table_ref, terms_ref, *refs):
    count = len(z.batches[number])
    pieces = refs[:count]
    out_ref, right_ref, sem = refs[count + 1 :]
    acc_ref = refs[count] if last else out_ref
    copies = []
    for at, piece in enumerate(pieces):
        copy = pltpu.make_async_copy(piece, right_ref.at[pl.ds(at * z.per, z.per)], sem.at[at])
        copy.start()
        copies.append(copy)
    for copy in copies:
        copy.wait()

    def field(entry, shift):
        return lax.shift_right_logical(entry, shift) & ((1 << AGG_BITS) - 1)

    def one_unit(unit, carry):
        parts = []
        for u in range(UNIT):
            entry = table_ref[z.entry_at + unit * UNIT + u]
            row = entry & ((1 << ROW_BITS) - 1)
            right = jnp.concatenate([right_ref[row, 0], right_ref[row, 1]], axis=1)
            value = jnp.dot(terms_ref[unit * UNIT + u], right, preferred_element_type=jnp.float32)
            aggs = [field(entry, ROW_BITS + n * AGG_BITS) for n in range(4)]
            parts.append((aggs, value))
        for aggs, value in parts:
            for a in range(2):
                for b in range(2):
                    acc_ref[aggs[a] * z.agg_cols + aggs[2 + b]] += value[
                        a * z.block : (a + 1) * z.block, b * z.block : (b + 1) * z.block
                    ]
        return carry

    begin = table_ref[z.start_at + number] // UNIT
    end = table_ref[z.start_at + number + 1] // UNIT
    lax.fori_loop(begin, end, one_unit, 0)
    if last:
        copy = pltpu.make_async_copy(
            acc_ref.at[pl.ds(0, z.agg_rows * z.agg_cols)], out_ref, sem.at[0]
        )
        copy.start()
        copy.wait()


def right_sums(z, number, pieces, table, terms, acc):
    count = len(pieces)
    last = number == len(z.batches) - 1
    if last:
        out_shape = jax.ShapeDtypeStruct(
            (z.agg_rows * z.agg_cols, z.block, z.block), jnp.float32
        )
    else:
        out_shape = pltpu.VMEM(z.acc_shape, jnp.float32)
    return pl.pallas_call(
        functools.partial(right_kernel, z, number, last),
        in_specs=[SMEM, VMEM] + [HBM] * count + [VMEM],
        out_specs=HBM if last else VMEM,
        out_shape=out_shape,
        scratch_shapes=[
            pltpu.VMEM((count * z.per, 2, z.block, z.block), jnp.bfloat16),
            pltpu.SemaphoreType.DMA((count,)),
        ],
        input_output_aliases={} if last else {2 + count: 0},
        compiler_params=pltpu.CompilerParams(vmem_limit_bytes=VMEM_LIMIT),
        cost_estimate=pl.CostEstimate(
            flops=count << 32, bytes_accessed=count * (32 << 20), transcendentals=0
        ),
        name="right_sums",
    )(table, in_vmem(terms), *pieces, in_vmem(acc))


def shards(stiffness, stiff_columns, stiff_stored, prolongator, prolong_columns):
    z = Sizes(stiffness, prolongator, lax.axis_size("row"), lax.axis_size("col"))
    bar = lax.optimization_barrier

    def across(x, d):
        return lax.ppermute(x, "col", [(c, c ^ d) for c in range(z.col_count)])

    def fetch(x, m):
        pairs = [
            ((c * z.ratio + k) * z.col_count + (q ^ c ^ m), (q * z.ratio + k) * z.col_count + c)
            for q in range(z.col_count)
            for k in range(z.ratio)
            for c in range(z.col_count)
        ]
        return lax.ppermute(x, ("row", "col"), pairs)

    def beside(x, j):
        return lax.ppermute(
            x, "row", [(r, r // z.ratio * z.ratio + (r + j) % z.ratio) for r in range(z.row_count)]
        )

    near = [d for d in range(1, z.col_count) if d & (d - 1) == 0]
    held = [across(prolongator, d) for d in near]
    right = {(m, 0): fetch(prolongator, m) for m in z.early}
    table, stiff, terms, acc = first_step(
        z, stiff_columns, stiff_stored, prolong_columns, stiffness, prolongator
    )
    table, *held = bar((table, *held))
    by = dict(zip(near, held))
    half = z.per // 2
    far = []
    for d in range(1, z.col_count):
        low = d & -d
        if d == low:
            continue
        if d ^ low in near:
            high = d ^ low
            far.append((d, [across(by[high][:half], low), across(by[low][half:], high)]))
        else:
            far.append((d, [across(prolongator, d)]))
    terms = left_terms(z, [(d, [by[d]]) for d in near], table, stiff, terms)
    again, table, *held = bar((prolongator, table, *right.values()))
    right = dict(zip(right, held))
    right |= {(m, 0): fetch(again, m) for m in z.late}
    others = range(1, z.ratio)
    right |= {(m, j): beside(right[m, 0], j) for m in z.early for j in others}
    terms = left_terms(z, far, table, stiff, terms)
    acc = right_sums(z, 0, [right[p] for p in z.batches[0]], table, terms, acc)
    table, *held = bar((table, *[right[m, 0] for m in z.late]))
    right |= {(m, 0): x for m, x in zip(z.late, held)}
    right |= {(m, j): beside(right[m, 0], j) for m in z.late for j in others}
    acc = right_sums(z, 1, [right[p] for p in z.batches[1]], table, terms, acc)
    coarse = right_sums(z, 2, [right[p] for p in z.batches[2]], table, terms, acc)
    return coarse.reshape(z.agg_rows, z.agg_cols, z.block, z.block)


def solution(mesh):
    return jax.shard_map(
        shards,
        mesh=mesh,
        in_specs=(
            P("row", "col", None, None),
            P("row", "col"),
            P("row", "col"),
            P(("row", "col"), None, None, None),
            P(),
        ),
        out_specs=P("row", "col", None, None),
        check_vma=False,
    )
```

time: 294 us -> 77.7 us (0.26)
  waiting for transfers between devices: 134 us -> 34.4 us
  matrix products: 70.7 us -> 0 us
  local copies, waits for them, and re-layouts: 63.9 us -> 3.13 us
  starting transfers between devices: 0.04 us -> 20.6 us
  Pallas kernels: 0 us -> 19.1 us
  between operations: 13.5 us -> 0.13 us
  other arithmetic: 8.81 us -> 0 us
    psum x1 -> x0, waiting for transfers between devices: 95.3 us -> none  [broadcast(): return lax.psum(kept, axis)]
    dot_general x8 -> x0, matrix products: 70.7 us -> none  [the longest x2 25.1 us: one_block(): jnp.einsum('iajxz,iak->kjxz', projected, left_onehot, precision=lax.Preci...]
    all_gather x1 -> x0, waiting for transfers between devices: 38.4 us -> none  [shards(): left_rows = lax.all_gather(prolongator, 'col', axis=0, tiled=True)]
    transpose x2 -> x0, local copies, waits for them, and re-layouts: 34.9 us -> none  [one_block(): jnp.einsum('iayx,ijyz->iajxz', left_block.astype(jnp.float32), collected,...]
    ppermute x0 -> x12, waiting for transfers between devices: none -> 34.4 us  [the longest x4 20.8 us: fetch(): return lax.ppermute(x, ('row', 'col'), pairs)]
    ppermute x0 -> x12, starting transfers between devices: none -> 20.6 us  [the longest x4 10.9 us: fetch(): return lax.ppermute(x, ('row', 'col'), pairs)]
    pallas_call x0 -> x6, Pallas kernels: none -> 19.1 us  [the longest x3 11.5 us: right_sums(): pl.pallas_call(functools.partial(right_kernel, z, number, last), in_specs...]
    convert_element_type x2 -> x0, local copies, waits for them, and re-layouts: 15.1 us -> none  [one_block(): (product * live_mask[:, :, None, None, None].astype(jnp.float32)).astype(...]
  transfers between devices with their start and end apart: 2 -> 12, of which waited for: 2 -> 6; matrix products, arithmetic and copies ran while one was open for 1% -> 0% of each run, Pallas kernels for 0% -> 19%
where the time goes in v2:
time: 77.7 us; the launch traced here: 77.4 us
  waiting for transfers between devices  34.4 us (44%)
  starting transfers between devices  20.6 us (27%)
  Pallas kernels  19.1 us (25%)
  local copies, waits for them, and re-layouts  3.13 us (4%)
    ppermute x4, waiting for transfers between devices, fetch(): return lax.ppermute(x, ('row', 'col'), pairs)  20.8 us
    ppermute x4, waiting for transfers between devices, across(): return lax.ppermute(x, 'col', [(c, c ^ d) for c in range(z.col_count)])  13.6 us
    pallas_call x3, Pallas kernels, right_sums(): pl.pallas_call(functools.partial(right_kernel, z, number, last), in_specs...  11.5 us
    ppermute x4, starting transfers between devices, fetch(): return lax.ppermute(x, ('row', 'col'), pairs)  10.9 us
    ppermute x4, starting transfers between devices, beside(): lax.ppermute(x, 'row', [(r, r // z.ratio * z.ratio + (r + j) % z.ratio) f...  5.44 us
    pallas_call x1, Pallas kernels, first_step(): pl.pallas_call(functools.partial(first_kernel, z), in_specs=[SMEM] * 3 +...  4.49 us
    ppermute x4, starting transfers between devices, across(): return lax.ppermute(x, 'col', [(c, c ^ d) for c in range(z.col_count)])  4.24 us
    pallas_call x2, Pallas kernels, left_terms(): pl.pallas_call(functools.partial(left_kernel, z, [(d, len(parts)) for d,...  3.14 us
  transfers between devices with their start and end apart: 12, of which 6 were waited for; matrix products, arithmetic and copies ran while one was open for 0% of the time, Pallas kernels for 19%

profile of v2, /device:TPU:5, one launch (start us, length us, event | category | flops | bytes accessed | tf_op | source)
XLA Modules:
  0.0 77.4 jit_solution(15702861422168008017)
XLA Ops:
  0.0 1.2 %collective-permute-start = (bf16[8,2,128,128]{3,2,1,0:T(8,128)(2,1)}, bf16[8,2,128,128]{3,2,1,0:T(8,128)(2,1)S(1)}, u32[]{:S(2)}, u32[]{:S(2)}) collective-permute-start(bf16[8,2,128,128]{3,2,1,0:T(8,128)(2,1)} %own_ref.1), channel_id=1, source_target_pairs={{0,1},{1,0},{2,3},{3,2},{4,5},{5,4},{6,7},{7,6},{8,9},{9,8},{10,11... | collective-permute-start | bytes 1572872 | tf_op jit(solution)/shard_map/ppermute | solution.py:289
  1.2 0.2 collective-permute-start.1
  1.4 5.2 %collective-permute-start.2 = (bf16[8,2,128,128]{3,2,1,0:T(8,128)(2,1)}, bf16[8,2,128,128]{3,2,1,0:T(8,128)(2,1)S(1)}, u32[]{:S(2)}, u32[]{:S(2)}) collective-permute-start(bf16[8,2,128,128]{3,2,1,0:T(8,128)(2,1)} %own_ref.1), channel_id=1, source_target_pairs={{0,0},{9,1},{18,2},{27,3},{4,4},{13,5},{22,6},{31,7},{1,8},{8,9},{... | collective-permute-start | bytes 1572872 | tf_op jit(solution)/shard_map/ppermute | solution.py:298
  6.6 1.9 %collective-permute-start.3 = (bf16[8,2,128,128]{3,2,1,0:T(8,128)(2,1)}, bf16[8,2,128,128]{3,2,1,0:T(8,128)(2,1)S(1)}, u32[]{:S(2)}, u32[]{:S(2)}) collective-permute-start(bf16[8,2,128,128]{3,2,1,0:T(8,128)(2,1)} %own_ref.1), channel_id=1, source_target_pairs={{3,0},{10,1},{17,2},{24,3},{7,4},{14,5},{21,6},{28,7},{2,8},{11,9}... | collective-permute-start | bytes 1572872 | tf_op jit(solution)/shard_map/ppermute | solution.py:298
  8.5 1.0 %copy-done = bf16[8,2,128,128]{3,2,1,0:T(8,128)(2,1)S(1)} copy-done((bf16[8,2,128,128]{3,2,1,0:T(8,128)(2,1)S(1)}, bf16[8,2,128,128]{3,2,1,0:T(8,128)(2,1)}, u32[]{:S(2)}) %copy-start) | copy-done | bytes 524312
  9.6 0.7 copy-done.1
  10.3 0.7 copy-done.2
  11.0 0.7 copy-done.3
  11.6 4.5 %first_step.1 = (s32[284]{0:T(512)S(1)}, bf16[32,4,128,128]{3,2,1,0:T(8,128)(2,1)S(1)}, bf16[153,256,128]{2,1,0:T(8,128)(2,1)S(1)}, f32[40,128,128]{2,1,0:T(8,128)S(1)}) custom-call(s32[4,32]{1,0:T(4,128)S(1)} %bitcast.4, s32[4,32]{1,0:T(4,128)S(1)} %bitcast.5, s32[2,256]{1,0:T(2,128)S(1)} %bitcast.6, bf16[32,4,128,128]{3,2,1,0:T(8,128)(2,1)} %stiff_ref.1, ...), custom_call_target="tpu_custom_call" | custom-call | flops 8589934592 | bytes 67108864 | tf_op jit(solution)/shard_map/first_step/pallas_call | solution.py:163
  16.1 3.6 %collective-permute-done.refs_0_ = bf16[8,2,128,128]{3,2,1,0:T(8,128)(2,1)S(1)} collective-permute-done((bf16[8,2,128,128]{3,2,1,0:T(8,128)(2,1)}, bf16[8,2,128,128]{3,2,1,0:T(8,128)(2,1)S(1)}, u32[]{:S(2)}, u32[]{:S(2)}) %collective-permute-start) | collective-permute-done | bytes 524320 | tf_op jit(solution)/shard_map/ppermute | solution.py:289
  19.8 0.0 collective-permute-done.1.refs_1_
  19.8 2.7 %collective-permute-start.6 = (bf16[4,2,128,128]{3,2,1,0:T(8,128)(2,1)S(1)}, bf16[4,2,128,128]{3,2,1,0:T(8,128)(2,1)S(1)}, u32[]{:S(2)}, u32[]{:S(2)}) collective-permute-start(bf16[4,2,128,128]{3,2,1,0:T(8,128)(2,1)S(1)} %slice.6), channel_id=1, source_target_pairs={{0,1},{1,0},{2,3},{3,2},{4,5},{5,4},{6,7},{7,6},{8,9},{9,8},{10,11... | collective-permute-start | bytes 786440 | tf_op jit(solution)/shard_map/ppermute | solution.py:289
  22.5 6.0 %collective-permute-done.2.refs_0_ = bf16[8,2,128,128]{3,2,1,0:T(8,128)(2,1)S(1)} collective-permute-done((bf16[8,2,128,128]{3,2,1,0:T(8,128)(2,1)}, bf16[8,2,128,128]{3,2,1,0:T(8,128)(2,1)S(1)}, u32[]{:S(2)}, u32[]{:S(2)}) %collective-permute-start.2) | collective-permute-done | bytes 524320 | tf_op jit(solution)/shard_map/ppermute | solution.py:298
  28.5 6.1 %collective-permute-done.3.refs_2_ = bf16[8,2,128,128]{3,2,1,0:T(8,128)(2,1)S(1)} collective-permute-done((bf16[8,2,128,128]{3,2,1,0:T(8,128)(2,1)}, bf16[8,2,128,128]{3,2,1,0:T(8,128)(2,1)S(1)}, u32[]{:S(2)}, u32[]{:S(2)}) %collective-permute-start.3) | collective-permute-done | bytes 524320 | tf_op jit(solution)/shard_map/ppermute | solution.py:298
  34.6 1.9 %collective-permute-start.4 = (bf16[8,2,128,128]{3,2,1,0:T(8,128)(2,1)S(1)}, bf16[8,2,128,128]{3,2,1,0:T(8,128)(2,1)S(1)}, u32[]{:S(2)}, u32[]{:S(2)}) collective-permute-start(bf16[8,2,128,128]{3,2,1,0:T(8,128)(2,1)S(1)} %copy-done), channel_id=1, source_target_pairs={{1,0},{8,1},{19,2},{26,3},{5,4},{12,5},{23,6},{30,7},{0,8},{9,9},{... | collective-permute-start | bytes 1572872 | tf_op jit(solution)/shard_map/ppermute | solution.py:298
  36.5 1.9 %collective-permute-start.5 = (bf16[8,2,128,128]{3,2,1,0:T(8,128)(2,1)S(1)}, bf16[8,2,128,128]{3,2,1,0:T(8,128)(2,1)S(1)}, u32[]{:S(2)}, u32[]{:S(2)}) collective-permute-start(bf16[8,2,128,128]{3,2,1,0:T(8,128)(2,1)S(1)} %copy-done), channel_id=1, source_target_pairs={{2,0},{11,1},{16,2},{25,3},{6,4},{15,5},{20,6},{29,7},{3,8},{10,9}... | collective-permute-start | bytes 1572872 | tf_op jit(solution)/shard_map/ppermute | solution.py:298
  38.5 0.1 collective-permute-start.7
  38.6 2.6 %collective-permute-start.10 = (bf16[8,2,128,128]{3,2,1,0:T(8,128)(2,1)S(1)}, bf16[8,2,128,128]{3,2,1,0:T(8,128)(2,1)S(1)}, u32[]{:S(2)}, u32[]{:S(2)}) collective-permute-start(bf16[8,2,128,128]{3,2,1,0:T(8,128)(2,1)S(1)} %collective-permute-done.2.refs_0_), channel_id=1, source_target_pairs={{0,4},{4,0},{8,12},{12,8},{16,20},{20,16},{24,28},{28,24},{1,5},{5... | collective-permute-start | bytes 1572872 | tf_op jit(solution)/shard_map/ppermute | solution.py:301
  41.2 0.0 collective-permute-done.6.refs_0_
  41.2 0.1 collective-permute-start.11
  41.2 1.8 %left_terms.2.refs_2_ = bf16[153,256,128]{2,1,0:T(8,128)(2,1)S(1)} custom-call(s32[284]{0:T(512)S(1)} %get-tuple-element.23.table_ref, bf16[32,4,128,128]{3,2,1,0:T(8,128)(2,1)S(1)} %get-tuple-element.24.held_ref, bf16[8,2,128,128]{3,2,1,0:T(8,128)(2,1)S(1)} %collective-permute-done.refs_0_, ...), custom_call_target="tpu_custom_call", output_to_operand_aliasing={{}: (4, {})} | custom-call | flops 8589934592 | bytes 67108864 | tf_op jit(solution)/shard_map/left_terms/pallas_call | solution.py:199
  43.1 10.0 %collective-permute-done.7.refs_1_ = bf16[4,2,128,128]{3,2,1,0:T(8,128)(2,1)S(1)} collective-permute-done((bf16[4,2,128,128]{3,2,1,0:T(8,128)(2,1)S(1)}, bf16[4,2,128,128]{3,2,1,0:T(8,128)(2,1)S(1)}, u32[]{:S(2)}, u32[]{:S(2)}) %collective-permute-start.7) | collective-permute-done | bytes 262176 | tf_op jit(solution)/shard_map/ppermute | solution.py:289
  53.1 1.3 %left_terms.3.terms_ref = bf16[153,256,128]{2,1,0:T(8,128)(2,1)S(1)} custom-call(s32[284]{0:T(512)S(1)} %get-tuple-element.23.table_ref, bf16[32,4,128,128]{3,2,1,0:T(8,128)(2,1)S(1)} %get-tuple-element.24.held_ref, bf16[4,2,128,128]{3,2,1,0:T(8,128)(2,1)S(1)} %collective-permute-done.6.refs_0_, ...), custom_call_target="tpu_custom_call", output_to_operand_aliasing={{}: (4, {})} | custom-call | flops 4294967296 | bytes 33554432 | tf_op jit(solution)/shard_map/left_terms/pallas_call | solution.py:199
  54.4 3.5 %collective-permute-done.4.refs_0_ = bf16[8,2,128,128]{3,2,1,0:T(8,128)(2,1)S(1)} collective-permute-done((bf16[8,2,128,128]{3,2,1,0:T(8,128)(2,1)S(1)}, bf16[8,2,128,128]{3,2,1,0:T(8,128)(2,1)S(1)}, u32[]{:S(2)}, u32[]{:S(2)}) %collective-permute-start.4) | collective-permute-done | bytes 524320 | tf_op jit(solution)/shard_map/ppermute | solution.py:298
  57.9 5.2 %collective-permute-done.5.refs_1_ = bf16[8,2,128,128]{3,2,1,0:T(8,128)(2,1)S(1)} collective-permute-done((bf16[8,2,128,128]{3,2,1,0:T(8,128)(2,1)S(1)}, bf16[8,2,128,128]{3,2,1,0:T(8,128)(2,1)S(1)}, u32[]{:S(2)}, u32[]{:S(2)}) %collective-permute-start.5) | collective-permute-done | bytes 524320 | tf_op jit(solution)/shard_map/ppermute | solution.py:298
  63.1 2.8 %collective-permute-start.8 = (bf16[8,2,128,128]{3,2,1,0:T(8,128)(2,1)S(1)}, bf16[8,2,128,128]{3,2,1,0:T(8,128)(2,1)S(1)}, u32[]{:S(2)}, u32[]{:S(2)}) collective-permute-start(bf16[8,2,128,128]{3,2,1,0:T(8,128)(2,1)S(1)} %collective-permute-done.4.refs_0_), channel_id=1, source_target_pairs={{0,4},{4,0},{8,12},{12,8},{16,20},{20,16},{24,28},{28,24},{1,5},{5... | collective-permute-start | bytes 1572872 | tf_op jit(solution)/shard_map/ppermute | solution.py:301
  65.9 0.0 collective-permute-start.9
  65.9 3.6 %right_sums.3.refs_2_ = f32[40,128,128]{2,1,0:T(8,128)S(1)} custom-call(s32[284]{0:T(512)S(1)} %get-tuple-element.23.table_ref, bf16[153,256,128]{2,1,0:T(8,128)(2,1)S(1)} %left_terms.3.terms_ref, bf16[8,2,128,128]{3,2,1,0:T(8,128)(2,1)S(1)} %collective-permute-done.2.refs_0_, ...), custom_call_target="tpu_custom_call", output_to_operand_aliasing={{}: (6, {})} | custom-call | flops 17179869184 | bytes 134217728 | tf_op jit(solution)/shard_map/right_sums/pallas_call | solution.py:266
  69.5 3.5 %right_sums.4.refs_2_ = f32[40,128,128]{2,1,0:T(8,128)S(1)} custom-call(s32[284]{0:T(512)S(1)} %get-tuple-element.23.table_ref, bf16[153,256,128]{2,1,0:T(8,128)(2,1)S(1)} %left_terms.3.terms_ref, bf16[8,2,128,128]{3,2,1,0:T(8,128)(2,1)S(1)} %collective-permute-done.4.refs_0_, ...), custom_call_target="tpu_custom_call", output_to_operand_aliasing={{}: (4, {})} | custom-call | flops 8589934592 | bytes 67108864 | tf_op jit(solution)/shard_map/right_sums/pallas_call | solution.py:266
  73.0 0.0 collective-permute-done.8.refs_0_
  73.0 0.0 collective-permute-done.9.refs_1_
  73.0 4.4 %right_sums.5 = f32[32,128,128]{2,1,0:T(8,128)} custom-call(s32[284]{0:T(512)S(1)} %get-tuple-element.23.table_ref, bf16[153,256,128]{2,1,0:T(8,128)(2,1)S(1)} %left_terms.3.terms_ref, bf16[8,2,128,128]{3,2,1,0:T(8,128)(2,1)S(1)} %collective-permute-done.8.refs_0_, bf16[8,2,128,128]{3,2,1,0:T(8,128)(2,1)S(1)} %collective-permute-done.9.refs_1_, ...), custom_call_target="tpu_custom_call" | custom-call | flops 8589934592 | bytes 67108864 | tf_op jit(solution)/shard_map/right_sums/pallas_call | solution.py:266
  (8 shorter events, 0.0 us)
Async XLA Ops:
  0.0 19.8 %collective-permute-start = (bf16[8,2,128,128]{3,2,1,0:T(8,128)(2,1)}, bf16[8,2,128,128]{3,2,1,0:T(8,128)(2,1)S(1)}, u32[]{:S(2)}, u32[]{:S(2)}) collective-permute-start(bf16[8,2,128,128]{3,2,1,0:T(8,128)(2,1)} %own_ref.1), channel_id=1, source_target_pairs={{0,1},{1,0},{2,3},{3,2},{4,5},{5,4},{6,7},{7,6},{8,9},{9,8},{10,11... | collective-permute-start | bytes 1572872 | tf_op jit(solution)/shard_map/ppermute | solution.py:289
  1.2 18.5 %collective-permute-start.1 = (bf16[8,2,128,128]{3,2,1,0:T(8,128)(2,1)}, bf16[8,2,128,128]{3,2,1,0:T(8,128)(2,1)S(1)}, u32[]{:S(2)}, u32[]{:S(2)}) collective-permute-start(bf16[8,2,128,128]{3,2,1,0:T(8,128)(2,1)} %own_ref.1), channel_id=1, source_target_pairs={{0,2},{1,3},{2,0},{3,1},{4,6},{5,7},{6,4},{7,5},{8,10},{9,11},{10,... | collective-permute-start | bytes 1572872 | tf_op jit(solution)/shard_map/ppermute | solution.py:289
  1.4 27.1 %collective-permute-start.2 = (bf16[8,2,128,128]{3,2,1,0:T(8,128)(2,1)}, bf16[8,2,128,128]{3,2,1,0:T(8,128)(2,1)S(1)}, u32[]{:S(2)}, u32[]{:S(2)}) collective-permute-start(bf16[8,2,128,128]{3,2,1,0:T(8,128)(2,1)} %own_ref.1), channel_id=1, source_target_pairs={{0,0},{9,1},{18,2},{27,3},{4,4},{13,5},{22,6},{31,7},{1,8},{8,9},{... | collective-permute-start | bytes 1572872 | tf_op jit(solution)/shard_map/ppermute | solution.py:298
  6.6 28.0 %collective-permute-start.3 = (bf16[8,2,128,128]{3,2,1,0:T(8,128)(2,1)}, bf16[8,2,128,128]{3,2,1,0:T(8,128)(2,1)S(1)}, u32[]{:S(2)}, u32[]{:S(2)}) collective-permute-start(bf16[8,2,128,128]{3,2,1,0:T(8,128)(2,1)} %own_ref.1), channel_id=1, source_target_pairs={{3,0},{10,1},{17,2},{24,3},{7,4},{14,5},{21,6},{28,7},{2,8},{11,9}... | collective-permute-start | bytes 1572872 | tf_op jit(solution)/shard_map/ppermute | solution.py:298
  8.5 1.1 %copy-start = (bf16[8,2,128,128]{3,2,1,0:T(8,128)(2,1)S(1)}, bf16[8,2,128,128]{3,2,1,0:T(8,128)(2,1)}, u32[]{:S(2)}) copy-start(bf16[8,2,128,128]{3,2,1,0:T(8,128)(2,1)} %own_ref.1) | copy-start | bytes 1572868
  9.6 0.7 copy-start.1
  10.3 0.7 copy-start.2
  11.0 0.7 copy-start.3
  19.8 21.4 %collective-permute-start.6 = (bf16[4,2,128,128]{3,2,1,0:T(8,128)(2,1)S(1)}, bf16[4,2,128,128]{3,2,1,0:T(8,128)(2,1)S(1)}, u32[]{:S(2)}, u32[]{:S(2)}) collective-permute-start(bf16[4,2,128,128]{3,2,1,0:T(8,128)(2,1)S(1)} %slice.6), channel_id=1, source_target_pairs={{0,1},{1,0},{2,3},{3,2},{4,5},{5,4},{6,7},{7,6},{8,9},{9,8},{10,11... | collective-permute-start | bytes 786440 | tf_op jit(solution)/shard_map/ppermute | solution.py:289
  34.6 23.3 %collective-permute-start.4 = (bf16[8,2,128,128]{3,2,1,0:T(8,128)(2,1)S(1)}, bf16[8,2,128,128]{3,2,1,0:T(8,128)(2,1)S(1)}, u32[]{:S(2)}, u32[]{:S(2)}) collective-permute-start(bf16[8,2,128,128]{3,2,1,0:T(8,128)(2,1)S(1)} %copy-done), channel_id=1, source_target_pairs={{1,0},{8,1},{19,2},{26,3},{5,4},{12,5},{23,6},{30,7},{0,8},{9,9},{... | collective-permute-start | bytes 1572872 | tf_op jit(solution)/shard_map/ppermute | solution.py:298
  36.5 26.5 %collective-permute-start.5 = (bf16[8,2,128,128]{3,2,1,0:T(8,128)(2,1)S(1)}, bf16[8,2,128,128]{3,2,1,0:T(8,128)(2,1)S(1)}, u32[]{:S(2)}, u32[]{:S(2)}) collective-permute-start(bf16[8,2,128,128]{3,2,1,0:T(8,128)(2,1)S(1)} %copy-done), channel_id=1, source_target_pairs={{2,0},{11,1},{16,2},{25,3},{6,4},{15,5},{20,6},{29,7},{3,8},{10,9}... | collective-permute-start | bytes 1572872 | tf_op jit(solution)/shard_map/ppermute | solution.py:298
  38.5 14.6 %collective-permute-start.7 = (bf16[4,2,128,128]{3,2,1,0:T(8,128)(2,1)S(1)}, bf16[4,2,128,128]{3,2,1,0:T(8,128)(2,1)S(1)}, u32[]{:S(2)}, u32[]{:S(2)}) collective-permute-start(bf16[4,2,128,128]{3,2,1,0:T(8,128)(2,1)S(1)} %slice.7), channel_id=1, source_target_pairs={{0,2},{1,3},{2,0},{3,1},{4,6},{5,7},{6,4},{7,5},{8,10},{9,11},{10,... | collective-permute-start | bytes 786440 | tf_op jit(solution)/shard_map/ppermute | solution.py:289
  38.6 27.3 %collective-permute-start.10 = (bf16[8,2,128,128]{3,2,1,0:T(8,128)(2,1)S(1)}, bf16[8,2,128,128]{3,2,1,0:T(8,128)(2,1)S(1)}, u32[]{:S(2)}, u32[]{:S(2)}) collective-permute-start(bf16[8,2,128,128]{3,2,1,0:T(8,128)(2,1)S(1)} %collective-permute-done.2.refs_0_), channel_id=1, source_target_pairs={{0,4},{4,0},{8,12},{12,8},{16,20},{20,16},{24,28},{28,24},{1,5},{5... | collective-permute-start | bytes 1572872 | tf_op jit(solution)/shard_map/ppermute | solution.py:301
  41.2 24.7 %collective-permute-start.11 = (bf16[8,2,128,128]{3,2,1,0:T(8,128)(2,1)S(1)}, bf16[8,2,128,128]{3,2,1,0:T(8,128)(2,1)S(1)}, u32[]{:S(2)}, u32[]{:S(2)}) collective-permute-start(bf16[8,2,128,128]{3,2,1,0:T(8,128)(2,1)S(1)} %collective-permute-done.3.refs_2_), channel_id=1, source_target_pairs={{0,4},{4,0},{8,12},{12,8},{16,20},{20,16},{24,28},{28,24},{1,5},{5... | collective-permute-start | bytes 1572872 | tf_op jit(solution)/shard_map/ppermute | solution.py:301
  63.1 9.9 %collective-permute-start.8 = (bf16[8,2,128,128]{3,2,1,0:T(8,128)(2,1)S(1)}, bf16[8,2,128,128]{3,2,1,0:T(8,128)(2,1)S(1)}, u32[]{:S(2)}, u32[]{:S(2)}) collective-permute-start(bf16[8,2,128,128]{3,2,1,0:T(8,128)(2,1)S(1)} %collective-permute-done.4.refs_0_), channel_id=1, source_target_pairs={{0,4},{4,0},{8,12},{12,8},{16,20},{20,16},{24,28},{28,24},{1,5},{5... | collective-permute-start | bytes 1572872 | tf_op jit(solution)/shard_map/ppermute | solution.py:301
  65.9 7.1 %collective-permute-start.9 = (bf16[8,2,128,128]{3,2,1,0:T(8,128)(2,1)S(1)}, bf16[8,2,128,128]{3,2,1,0:T(8,128)(2,1)S(1)}, u32[]{:S(2)}, u32[]{:S(2)}) collective-permute-start(bf16[8,2,128,128]{3,2,1,0:T(8,128)(2,1)S(1)} %collective-permute-done.5.refs_1_), channel_id=1, source_target_pairs={{0,4},{4,0},{8,12},{12,8},{16,20},{20,16},{24,28},{28,24},{1,5},{5... | collective-permute-start | bytes 1572872 | tf_op jit(solution)/shard_map/ppermute | solution.py:301

commit v3 on v2

--- a/solution.py
+++ b/solution.py
@@ -8,7 +8,7 @@
 from jax.sharding import PartitionSpec as P
 
 G = 8
-UNIT = 8
+UNIT = 16
 VMEM_LIMIT = 16 << 20
 HBM = pl.BlockSpec(memory_space=pltpu.HBM)
 SMEM = pl.BlockSpec(memory_space=pltpu.SMEM)
@@ -308,28 +308,21 @@
     table, stiff, terms, acc = first_step(
         z, stiff_columns, stiff_stored, prolong_columns, stiffness, prolongator
     )
-    table, *held = bar((table, *held))
+    again, table = bar((prolongator, table))
     by = dict(zip(near, held))
-    half = z.per // 2
-    far = []
+    far = {}
     for d in range(1, z.col_count):
+        if d in near:
+            continue
         low = d & -d
-        if d == low:
-            continue
-        if d ^ low in near:
-            high = d ^ low
-            far.append((d, [across(by[high][:half], low), across(by[low][half:], high)]))
-        else:
-            far.append((d, [across(prolongator, d)]))
+        far[d] = across(by[d ^ low], low) if d ^ low in near else across(again, d)
+    right |= {(m, 0): fetch(again, m) for m in z.late}
     terms = left_terms(z, [(d, [by[d]]) for d in near], table, stiff, terms)
-    again, table, *held = bar((prolongator, table, *right.values()))
-    right = dict(zip(right, held))
-    right |= {(m, 0): fetch(again, m) for m in z.late}
+    terms = left_terms(z, [(d, [x]) for d, x in far.items()], table, stiff, terms)
     others = range(1, z.ratio)
     right |= {(m, j): beside(right[m, 0], j) for m in z.early for j in others}
-    terms = left_terms(z, far, table, stiff, terms)
     acc = right_sums(z, 0, [right[p] for p in z.batches[0]], table, terms, acc)
-    table, *held = bar((table, *[right[m, 0] for m in z.late]))
+    acc, *held = bar((acc, *[right[m, 0] for m in z.late]))
     right |= {(m, 0): x for m, x in zip(z.late, held)}
     right |= {(m, j): beside(right[m, 0], j) for m in z.late for j in others}
     acc = right_sums(z, 1, [right[p] for p in z.batches[1]], table, terms, acc)

time: 77.7 us -> 71.1 us (0.915)
  the two profiles are of different devices: /device:TPU:5 before, /device:TPU:12 now
where the time goes in v3:
time: 71.1 us
  waiting for transfers between devices  28.4 us (40%)
  starting transfers between devices  20.3 us (29%)
  Pallas kernels  19.2 us (27%)
  local copies, waits for them, and re-layouts  3.09 us (4%)
    ppermute x4, waiting for transfers between devices, fetch(): return lax.ppermute(x, ('row', 'col'), pairs)  20.2 us
    ppermute x4, starting transfers between devices, fetch(): return lax.ppermute(x, ('row', 'col'), pairs)  14.9 us
    pallas_call x3, Pallas kernels, right_sums(): pl.pallas_call(functools.partial(right_kernel, z, number, last), in_specs...  11.6 us
    ppermute x3, waiting for transfers between devices, across(): return lax.ppermute(x, 'col', [(c, c ^ d) for c in range(z.col_count)])  8.17 us
    pallas_call x1, Pallas kernels, first_step(): pl.pallas_call(functools.partial(first_kernel, z), in_specs=[SMEM] * 3 +...  4.5 us
    ppermute x3, starting transfers between devices, across(): return lax.ppermute(x, 'col', [(c, c ^ d) for c in range(z.col_count)])  4.37 us
    pallas_call x2, Pallas kernels, left_terms(): pl.pallas_call(functools.partial(left_kernel, z, [(d, len(parts)) for d,...  3.14 us
    unnamed x8, local copies, waits for them, and re-layouts  3.09 us
  transfers between devices with their start and end apart: 11, of which 3 were waited for; matrix products, arithmetic and copies ran while one was open for 0% of the time, Pallas kernels for 21%

profile of v3, /device:TPU:12, one launch (start us, length us, event | category | flops | bytes accessed | tf_op | source)
XLA Modules:
  0.0 71.1 jit_solution(12363146932653919379)
XLA Ops:
  0.0 0.5 collective-permute-start
  0.5 1.5 %collective-permute-start.2 = (bf16[8,2,128,128]{3,2,1,0:T(8,128)(2,1)}, bf16[8,2,128,128]{3,2,1,0:T(8,128)(2,1)S(1)}, u32[]{:S(2)}, u32[]{:S(2)}) collective-permute-start(bf16[8,2,128,128]{3,2,1,0:T(8,128)(2,1)} %own_ref.1), channel_id=1, source_target_pairs={{0,1},{1,0},{2,3},{3,2},{4,5},{5,4},{6,7},{7,6},{8,9},{9,8},{10,11... | collective-permute-start | bytes 1572872 | tf_op jit(solution)/shard_map/ppermute | solution.py:289
  2.0 5.4 %collective-permute-start.3 = (bf16[8,2,128,128]{3,2,1,0:T(8,128)(2,1)}, bf16[8,2,128,128]{3,2,1,0:T(8,128)(2,1)S(1)}, u32[]{:S(2)}, u32[]{:S(2)}) collective-permute-start(bf16[8,2,128,128]{3,2,1,0:T(8,128)(2,1)} %own_ref.1), channel_id=1, source_target_pairs={{0,0},{9,1},{18,2},{27,3},{4,4},{13,5},{22,6},{31,7},{1,8},{8,9},{... | collective-permute-start | bytes 1572872 | tf_op jit(solution)/shard_map/ppermute | solution.py:298
  7.4 2.3 %collective-permute-start.5 = (bf16[8,2,128,128]{3,2,1,0:T(8,128)(2,1)}, bf16[8,2,128,128]{3,2,1,0:T(8,128)(2,1)S(1)}, u32[]{:S(2)}, u32[]{:S(2)}) collective-permute-start(bf16[8,2,128,128]{3,2,1,0:T(8,128)(2,1)} %own_ref.1), channel_id=1, source_target_pairs={{3,0},{10,1},{17,2},{24,3},{7,4},{14,5},{21,6},{28,7},{2,8},{11,9}... | collective-permute-start | bytes 1572872 | tf_op jit(solution)/shard_map/ppermute | solution.py:298
  9.7 1.0 %copy-done = bf16[8,2,128,128]{3,2,1,0:T(8,128)(2,1)S(1)} copy-done((bf16[8,2,128,128]{3,2,1,0:T(8,128)(2,1)S(1)}, bf16[8,2,128,128]{3,2,1,0:T(8,128)(2,1)}, u32[]{:S(2)}) %copy-start) | copy-done | bytes 524312
  10.8 0.7 copy-done.1
  11.4 0.7 copy-done.2
  12.1 0.7 copy-done.3
  12.8 4.5 %first_step.1 = (s32[308]{0:T(512)S(1)}, bf16[32,4,128,128]{3,2,1,0:T(8,128)(2,1)S(1)}, bf16[177,256,128]{2,1,0:T(8,128)(2,1)S(1)}, f32[40,128,128]{2,1,0:T(8,128)S(1)}) custom-call(s32[4,32]{1,0:T(4,128)S(1)} %bitcast.4, s32[4,32]{1,0:T(4,128)S(1)} %bitcast.5, s32[2,256]{1,0:T(2,128)S(1)} %bitcast.6, bf16[32,4,128,128]{3,2,1,0:T(8,128)(2,1)} %stiff_ref.1, ...), custom_call_target="tpu_custom_call" | custom-call | flops 8589934592 | bytes 67108864 | tf_op jit(solution)/shard_map/first_step/pallas_call | solution.py:163
  17.3 5.3 %collective-permute-start.7 = (bf16[8,2,128,128]{3,2,1,0:T(8,128)(2,1)S(1)}, bf16[8,2,128,128]{3,2,1,0:T(8,128)(2,1)S(1)}, u32[]{:S(2)}, u32[]{:S(2)}) collective-permute-start(bf16[8,2,128,128]{3,2,1,0:T(8,128)(2,1)S(1)} %copy-done), channel_id=1, source_target_pairs={{1,0},{8,1},{19,2},{26,3},{5,4},{12,5},{23,6},{30,7},{0,8},{9,9},{... | collective-permute-start | bytes 1572872 | tf_op jit(solution)/shard_map/ppermute | solution.py:298
  22.6 0.0 collective-permute-done.refs_1_
  22.6 1.9 %collective-permute-start.8 = (bf16[8,2,128,128]{3,2,1,0:T(8,128)(2,1)S(1)}, bf16[8,2,128,128]{3,2,1,0:T(8,128)(2,1)S(1)}, u32[]{:S(2)}, u32[]{:S(2)}) collective-permute-start(bf16[8,2,128,128]{3,2,1,0:T(8,128)(2,1)S(1)} %copy-done), channel_id=1, source_target_pairs={{2,0},{11,1},{16,2},{25,3},{6,4},{15,5},{20,6},{29,7},{3,8},{10,9}... | collective-permute-start | bytes 1572872 | tf_op jit(solution)/shard_map/ppermute | solution.py:298
  24.5 0.8 %collective-permute-done.2.refs_0_ = bf16[8,2,128,128]{3,2,1,0:T(8,128)(2,1)S(1)} collective-permute-done((bf16[8,2,128,128]{3,2,1,0:T(8,128)(2,1)}, bf16[8,2,128,128]{3,2,1,0:T(8,128)(2,1)S(1)}, u32[]{:S(2)}, u32[]{:S(2)}) %collective-permute-start.2) | collective-permute-done | bytes 524320 | tf_op jit(solution)/shard_map/ppermute | solution.py:289
  25.4 2.4 %collective-permute-start.1 = (bf16[8,2,128,128]{3,2,1,0:T(8,128)(2,1)S(1)}, bf16[8,2,128,128]{3,2,1,0:T(8,128)(2,1)S(1)}, u32[]{:S(2)}, u32[]{:S(2)}) collective-permute-start(bf16[8,2,128,128]{3,2,1,0:T(8,128)(2,1)S(1)} %collective-permute-done.refs_1_), channel_id=1, source_target_pairs={{0,1},{1,0},{2,3},{3,2},{4,5},{5,4},{6,7},{7,6},{8,9},{9,8},{10,11... | collective-permute-start | bytes 1572872 | tf_op jit(solution)/shard_map/ppermute | solution.py:289
  27.8 20.2 %collective-permute-done.3.refs_0_ = bf16[8,2,128,128]{3,2,1,0:T(8,128)(2,1)S(1)} collective-permute-done((bf16[8,2,128,128]{3,2,1,0:T(8,128)(2,1)}, bf16[8,2,128,128]{3,2,1,0:T(8,128)(2,1)S(1)}, u32[]{:S(2)}, u32[]{:S(2)}) %collective-permute-start.3) | collective-permute-done | bytes 524320 | tf_op jit(solution)/shard_map/ppermute | solution.py:298
  47.9 0.0 collective-permute-start.4
  47.9 0.0 collective-permute-done.5.refs_2_
  47.9 0.5 collective-permute-start.6
  48.5 1.8 %left_terms.2.refs_1_ = bf16[177,256,128]{2,1,0:T(8,128)(2,1)S(1)} custom-call(s32[308]{0:T(512)S(1)} %get-tuple-element.15.table_ref, bf16[32,4,128,128]{3,2,1,0:T(8,128)(2,1)S(1)} %get-tuple-element.16.held_ref, bf16[8,2,128,128]{3,2,1,0:T(8,128)(2,1)S(1)} %collective-permute-done.2.refs_0_, ...), custom_call_target="tpu_custom_call", output_to_operand_aliasing={{}: (4, {})} | custom-call | flops 8589934592 | bytes 67108864 | tf_op jit(solution)/shard_map/left_terms/pallas_call | solution.py:199
  50.3 7.3 %collective-permute-done.1.refs_0_ = bf16[8,2,128,128]{3,2,1,0:T(8,128)(2,1)S(1)} collective-permute-done((bf16[8,2,128,128]{3,2,1,0:T(8,128)(2,1)S(1)}, bf16[8,2,128,128]{3,2,1,0:T(8,128)(2,1)S(1)}, u32[]{:S(2)}, u32[]{:S(2)}) %collective-permute-start.1) | collective-permute-done | bytes 524320 | tf_op jit(solution)/shard_map/ppermute | solution.py:289
  57.6 1.3 %left_terms.3.terms_ref = bf16[177,256,128]{2,1,0:T(8,128)(2,1)S(1)} custom-call(s32[308]{0:T(512)S(1)} %get-tuple-element.15.table_ref, bf16[32,4,128,128]{3,2,1,0:T(8,128)(2,1)S(1)} %get-tuple-element.16.held_ref, bf16[8,2,128,128]{3,2,1,0:T(8,128)(2,1)S(1)} %collective-permute-done.1.refs_0_, ...), custom_call_target="tpu_custom_call", output_to_operand_aliasing={{}: (3, {})} | custom-call | flops 4294967296 | bytes 33554432 | tf_op jit(solution)/shard_map/left_terms/pallas_call | solution.py:199
  58.9 0.0 collective-permute-done.4.refs_1_
  58.9 0.0 collective-permute-done.6.refs_3_
  59.0 4.0 %right_sums.3.refs_2_ = f32[40,128,128]{2,1,0:T(8,128)S(1)} custom-call(s32[308]{0:T(512)S(1)} %get-tuple-element.15.table_ref, bf16[177,256,128]{2,1,0:T(8,128)(2,1)S(1)} %left_terms.3.terms_ref, bf16[8,2,128,128]{3,2,1,0:T(8,128)(2,1)S(1)} %collective-permute-done.3.refs_0_, ...), custom_call_target="tpu_custom_call", output_to_operand_aliasing={{}: (6, {})} | custom-call | flops 17179869184 | bytes 134217728 | tf_op jit(solution)/shard_map/right_sums/pallas_call | solution.py:266
  63.0 0.0 collective-permute-done.7.refs_0_
  63.0 0.0 collective-permute-done.8.refs_1_
  63.0 0.1 collective-permute-start.10
  63.1 0.5 collective-permute-start.9
  63.6 3.1 %right_sums.4.refs_2_ = f32[40,128,128]{2,1,0:T(8,128)S(1)} custom-call(s32[308]{0:T(512)S(1)} %get-tuple-element.15.table_ref, bf16[177,256,128]{2,1,0:T(8,128)(2,1)S(1)} %left_terms.3.terms_ref, bf16[8,2,128,128]{3,2,1,0:T(8,128)(2,1)S(1)} %collective-permute-done.7.refs_0_, ...), custom_call_target="tpu_custom_call", output_to_operand_aliasing={{}: (4, {})} | custom-call | flops 8589934592 | bytes 67108864 | tf_op jit(solution)/shard_map/right_sums/pallas_call | solution.py:266
  66.7 0.0 collective-permute-done.10.refs_1_
  66.7 0.0 collective-permute-done.9.refs_0_
  66.7 4.4 %right_sums.5 = f32[32,128,128]{2,1,0:T(8,128)} custom-call(s32[308]{0:T(512)S(1)} %get-tuple-element.15.table_ref, bf16[177,256,128]{2,1,0:T(8,128)(2,1)S(1)} %left_terms.3.terms_ref, bf16[8,2,128,128]{3,2,1,0:T(8,128)(2,1)S(1)} %collective-permute-done.9.refs_0_, bf16[8,2,128,128]{3,2,1,0:T(8,128)(2,1)S(1)} %collective-permute-done.10.refs_1_, ...), custom_call_target="tpu_custom_call" | custom-call | flops 8589934592 | bytes 67108864 | tf_op jit(solution)/shard_map/right_sums/pallas_call | solution.py:266
  (4 shorter events, 0.0 us)
Async XLA Ops:
  0.0 22.6 %collective-permute-start = (bf16[8,2,128,128]{3,2,1,0:T(8,128)(2,1)}, bf16[8,2,128,128]{3,2,1,0:T(8,128)(2,1)S(1)}, u32[]{:S(2)}, u32[]{:S(2)}) collective-permute-start(bf16[8,2,128,128]{3,2,1,0:T(8,128)(2,1)} %own_ref.1), channel_id=1, source_target_pairs={{0,2},{1,3},{2,0},{3,1},{4,6},{5,7},{6,4},{7,5},{8,10},{9,11},{10,... | collective-permute-start | bytes 1572872 | tf_op jit(solution)/shard_map/ppermute | solution.py:289
  0.5 24.9 %collective-permute-start.2 = (bf16[8,2,128,128]{3,2,1,0:T(8,128)(2,1)}, bf16[8,2,128,128]{3,2,1,0:T(8,128)(2,1)S(1)}, u32[]{:S(2)}, u32[]{:S(2)}) collective-permute-start(bf16[8,2,128,128]{3,2,1,0:T(8,128)(2,1)} %own_ref.1), channel_id=1, source_target_pairs={{0,1},{1,0},{2,3},{3,2},{4,5},{5,4},{6,7},{7,6},{8,9},{9,8},{10,11... | collective-permute-start | bytes 1572872 | tf_op jit(solution)/shard_map/ppermute | solution.py:289
  2.0 45.9 %collective-permute-start.3 = (bf16[8,2,128,128]{3,2,1,0:T(8,128)(2,1)}, bf16[8,2,128,128]{3,2,1,0:T(8,128)(2,1)S(1)}, u32[]{:S(2)}, u32[]{:S(2)}) collective-permute-start(bf16[8,2,128,128]{3,2,1,0:T(8,128)(2,1)} %own_ref.1), channel_id=1, source_target_pairs={{0,0},{9,1},{18,2},{27,3},{4,4},{13,5},{22,6},{31,7},{1,8},{8,9},{... | collective-permute-start | bytes 1572872 | tf_op jit(solution)/shard_map/ppermute | solution.py:298
  7.4 40.5 %collective-permute-start.5 = (bf16[8,2,128,128]{3,2,1,0:T(8,128)(2,1)}, bf16[8,2,128,128]{3,2,1,0:T(8,128)(2,1)S(1)}, u32[]{:S(2)}, u32[]{:S(2)}) collective-permute-start(bf16[8,2,128,128]{3,2,1,0:T(8,128)(2,1)} %own_ref.1), channel_id=1, source_target_pairs={{3,0},{10,1},{17,2},{24,3},{7,4},{14,5},{21,6},{28,7},{2,8},{11,9}... | collective-permute-start | bytes 1572872 | tf_op jit(solution)/shard_map/ppermute | solution.py:298
  9.7 1.1 %copy-start = (bf16[8,2,128,128]{3,2,1,0:T(8,128)(2,1)S(1)}, bf16[8,2,128,128]{3,2,1,0:T(8,128)(2,1)}, u32[]{:S(2)}) copy-start(bf16[8,2,128,128]{3,2,1,0:T(8,128)(2,1)} %own_ref.1) | copy-start | bytes 1572868
  10.8 0.7 copy-start.1
  11.4 0.7 copy-start.2
  12.1 0.7 copy-start.3
  17.3 45.7 %collective-permute-start.7 = (bf16[8,2,128,128]{3,2,1,0:T(8,128)(2,1)S(1)}, bf16[8,2,128,128]{3,2,1,0:T(8,128)(2,1)S(1)}, u32[]{:S(2)}, u32[]{:S(2)}) collective-permute-start(bf16[8,2,128,128]{3,2,1,0:T(8,128)(2,1)S(1)} %copy-done), channel_id=1, source_target_pairs={{1,0},{8,1},{19,2},{26,3},{5,4},{12,5},{23,6},{30,7},{0,8},{9,9},{... | collective-permute-start | bytes 1572872 | tf_op jit(solution)/shard_map/ppermute | solution.py:298
  22.6 40.4 %collective-permute-start.8 = (bf16[8,2,128,128]{3,2,1,0:T(8,128)(2,1)S(1)}, bf16[8,2,128,128]{3,2,1,0:T(8,128)(2,1)S(1)}, u32[]{:S(2)}, u32[]{:S(2)}) collective-permute-start(bf16[8,2,128,128]{3,2,1,0:T(8,128)(2,1)S(1)} %copy-done), channel_id=1, source_target_pairs={{2,0},{11,1},{16,2},{25,3},{6,4},{15,5},{20,6},{29,7},{3,8},{10,9}... | collective-permute-start | bytes 1572872 | tf_op jit(solution)/shard_map/ppermute | solution.py:298
  25.4 32.2 %collective-permute-start.1 = (bf16[8,2,128,128]{3,2,1,0:T(8,128)(2,1)S(1)}, bf16[8,2,128,128]{3,2,1,0:T(8,128)(2,1)S(1)}, u32[]{:S(2)}, u32[]{:S(2)}) collective-permute-start(bf16[8,2,128,128]{3,2,1,0:T(8,128)(2,1)S(1)} %collective-permute-done.refs_1_), channel_id=1, source_target_pairs={{0,1},{1,0},{2,3},{3,2},{4,5},{5,4},{6,7},{7,6},{8,9},{9,8},{10,11... | collective-permute-start | bytes 1572872 | tf_op jit(solution)/shard_map/ppermute | solution.py:289
  47.9 11.0 %collective-permute-start.4 = (bf16[8,2,128,128]{3,2,1,0:T(8,128)(2,1)S(1)}, bf16[8,2,128,128]{3,2,1,0:T(8,128)(2,1)S(1)}, u32[]{:S(2)}, u32[]{:S(2)}) collective-permute-start(bf16[8,2,128,128]{3,2,1,0:T(8,128)(2,1)S(1)} %collective-permute-done.3.refs_0_), channel_id=1, source_target_pairs={{0,4},{4,0},{8,12},{12,8},{16,20},{20,16},{24,28},{28,24},{1,5},{5... | collective-permute-start | bytes 1572872 | tf_op jit(solution)/shard_map/ppermute | solution.py:301
  47.9 11.0 %collective-permute-start.6 = (bf16[8,2,128,128]{3,2,1,0:T(8,128)(2,1)S(1)}, bf16[8,2,128,128]{3,2,1,0:T(8,128)(2,1)S(1)}, u32[]{:S(2)}, u32[]{:S(2)}) collective-permute-start(bf16[8,2,128,128]{3,2,1,0:T(8,128)(2,1)S(1)} %collective-permute-done.5.refs_2_), channel_id=1, source_target_pairs={{0,4},{4,0},{8,12},{12,8},{16,20},{20,16},{24,28},{28,24},{1,5},{5... | collective-permute-start | bytes 1572872 | tf_op jit(solution)/shard_map/ppermute | solution.py:301
  63.0 3.7 %collective-permute-start.10 = (bf16[8,2,128,128]{3,2,1,0:T(8,128)(2,1)S(1)}, bf16[8,2,128,128]{3,2,1,0:T(8,128)(2,1)S(1)}, u32[]{:S(2)}, u32[]{:S(2)}) collective-permute-start(bf16[8,2,128,128]{3,2,1,0:T(8,128)(2,1)S(1)} %collective-permute-done.8.refs_1_), channel_id=1, source_target_pairs={{0,4},{4,0},{8,12},{12,8},{16,20},{20,16},{24,28},{28,24},{1,5},{5... | collective-permute-start | bytes 1572872 | tf_op jit(solution)/shard_map/ppermute | solution.py:301
  63.1 3.6 %collective-permute-start.9 = (bf16[8,2,128,128]{3,2,1,0:T(8,128)(2,1)S(1)}, bf16[8,2,128,128]{3,2,1,0:T(8,128)(2,1)S(1)}, u32[]{:S(2)}, u32[]{:S(2)}) collective-permute-start(bf16[8,2,128,128]{3,2,1,0:T(8,128)(2,1)S(1)} %collective-permute-done.7.refs_0_), channel_id=1, source_target_pairs={{0,4},{4,0},{8,12},{12,8},{16,20},{20,16},{24,28},{28,24},{1,5},{5... | collective-permute-start | bytes 1572872 | tf_op jit(solution)/shard_map/ppermute | solution.py:301
